TPU v7x, 512 devices: a whole 4x8x8 slice. The times are simulated.
512 devices in a mesh: ctx: 128 (over x_hi, y, z), head: 4 (over x_lo, core).
Axes of the slice: x: 4 (x_hi: 2, x_lo: 2; x = x_hi * 2 + x_lo), y: 8, z: 8, core: 2. Of those that a mesh axis runs over, the one named last changes fastest.
Arguments:
- queries: bfloat16 [16384, 2048], P('ctx', 'head'), may hold values from -6 to 6
- new_keys: bfloat16 [16384, 128], P('ctx'), may hold values from -6 to 6
- new_values: bfloat16 [16384, 128], P('ctx'), may hold values from -6 to 6
- cache_keys: bfloat16 [8192, 128], P('ctx'), may hold values from -9 to 9
- cache_values: bfloat16 [8192, 128], P('ctx'), may hold values from -6 to 6
- q_request: int32 [16384], replicated, may hold values from 0 to 3, never falling along the last dimension, each value on 1 to 8192 neighbouring positions
- block_request: int32 [512], replicated, may hold values from 0 to 3
Outputs:
- attention: bfloat16 [16384, 2048], P('ctx', 'head')
Inputs may be any that keep to these rules, and one draw needn't show every extreme that they name: `q_request`: request numbers never fall along the rows; each of the 4 requests has one row or more, and one has exactly 8192.
All inputs are finite; a program needn't handle non-finite values.
Results may differ from a plain program's by a relative error of at most 0.006.
Values may be sent and summed in bfloat16 or wider, within the bound.
No kernel may reach another device: no remote copies, remote signals or barrier semaphores. Data moves between devices by JAX's collectives and lax.ppermute only.
A program may use at most 64 MiB of HBM per device.

v0:
```python
import jax
import jax.numpy as jnp
from jax import lax
from jax.sharding import PartitionSpec as P

HD = 128
BLK = 16


masked_score = -1e30


def attend(carry_state, query_rows, key_rows, value_rows, allowed):
    running_max, weight_sum, output_sum = carry_state
    scores = jnp.einsum(
        "qhd,kd->hqk", query_rows, key_rows, preferred_element_type=jnp.float32
    ) * HD ** (-0.5)
    scores = jnp.where(allowed[None], scores, masked_score)
    new_max = jnp.maximum(running_max, jnp.max(scores, axis=-1))
    factor = jnp.exp(running_max - new_max)
    weights = jnp.where(allowed[None], jnp.exp(scores - new_max[..., None]), 0.0)
    weight_sum = weight_sum * factor + jnp.sum(weights, axis=-1)
    output_sum = output_sum * factor[..., None] + jnp.einsum(
        "hqk,kd->hqd", weights.astype(jnp.bfloat16), value_rows, preferred_element_type=jnp.float32
    )
    return (new_max, weight_sum, output_sum)


def sweep_keys(
    carry_state,
    query_rows,
    row_requests,
    row_positions,
    key_rows,
    value_rows,
    key_requests,
    key_positions,
):
    key_count = key_rows.shape[0]
    block_width = 512

    def one_step(inner_state, block_number):
        lower = block_number * block_width
        keys_here = lax.dynamic_slice_in_dim(key_rows, lower, block_width, 0)
        values_here = lax.dynamic_slice_in_dim(value_rows, lower, block_width, 0)
        requests_here = lax.dynamic_slice_in_dim(key_requests, lower, block_width, 0)
        positions_here = lax.dynamic_slice_in_dim(key_positions, lower, block_width, 0)
        allowed = (row_requests[:, None] == requests_here[None, :]) & (
            positions_here[None, :] <= row_positions[:, None]
        )
        return (attend(inner_state, query_rows, keys_here, values_here, allowed), None)

    carry_state, unused = lax.scan(
        one_step, carry_state, jnp.arange(key_count // block_width, dtype=jnp.int32)
    )
    return carry_state


def body(queries, new_keys, new_values, cache_keys, cache_values, q_request, block_request):
    local_rows = queries.shape[0]
    heads_here = queries.shape[1] // HD
    first_row = lax.axis_index("ctx") * local_rows
    row_positions = first_row + jnp.arange(local_rows, dtype=jnp.int32)
    row_requests = lax.dynamic_slice_in_dim(q_request, first_row, local_rows, 0)
    new_pair = (new_keys, new_values)
    cache_pair = (cache_keys, cache_values)
    own_rows = queries.reshape(local_rows, heads_here, HD)
    count_heads = own_rows.shape[1]
    start_state = (
        jnp.full((count_heads, local_rows), masked_score, jnp.float32),
        jnp.zeros((count_heads, local_rows), jnp.float32),
        jnp.zeros((count_heads, local_rows, HD), jnp.float32),
    )
    key_rows = lax.all_gather(cache_pair[0], "ctx", axis=0, tiled=True)
    value_rows = lax.all_gather(cache_pair[1], "ctx", axis=0, tiled=True)
    global_rows = jnp.arange(key_rows.shape[0], dtype=jnp.int32)
    key_requests = block_request[global_rows // BLK]
    key_positions = jnp.full((key_rows.shape[0],), -1, jnp.int32)
    carry_state = sweep_keys(
        start_state,
        own_rows,
        row_requests,
        row_positions,
        key_rows,
        value_rows,
        key_requests,
        key_positions,
    )
    key_rows = lax.all_gather(new_pair[0], "ctx", axis=0, tiled=True)
    value_rows = lax.all_gather(new_pair[1], "ctx", axis=0, tiled=True)
    key_positions = jnp.arange(key_rows.shape[0], dtype=jnp.int32)
    key_requests = q_request[key_positions]
    carry_state = sweep_keys(
        carry_state,
        own_rows,
        row_requests,
        row_positions,
        key_rows,
        value_rows,
        key_requests,
        key_positions,
    )
    running_max, weight_sum, output_sum = carry_state
    result = output_sum / weight_sum[..., None]
    return (
        jnp.transpose(result, (1, 0, 2)).reshape(local_rows, heads_here * HD).astype(jnp.bfloat16)
    )


def solution(mesh):
    return jax.shard_map(
        body,
        mesh=mesh,
        in_specs=(
            P("ctx", "head"),
            P("ctx", None),
            P("ctx", None),
            P("ctx", None),
            P("ctx", None),
            P(),
            P(),
        ),
        out_specs=P("ctx", "head"),
        check_vma=False,
    )
```

profile of v0, /device:TPU:56, one launch (start us, length us, event | category | flops | bytes accessed | tf_op | source)
XLA Modules:
  0.0 698.6 jit_solution(11070878009881982266)
XLA Ops:
  11.4 90.5 %gather_fusion.1 = s32[16384]{0:T(1024)S(1)} fusion(s32[16384]{0:T(1024)S(1)} %copy-done.1, s32[16384]{0:T(1024)S(1)} %iota_clamp_fusion), kind=kCustom, calls=%fused_computation.1 | custom fusion | bytes 196608 | tf_op jit(solution)/shard_map/gather | solution.py:92
  101.9 51.2 %gather_fusion = s32[8192]{0:T(1024)S(1)} fusion(s32[512]{0:T(512)S(1)} %copy-done, s32[8192]{0:T(1024)S(1)} %broadcast_clamp_fusion), kind=kCustom, calls=%fused_computation | custom fusion | bytes 98304 | tf_op jit(solution)/shard_map/gather | solution.py:77
  153.1 118.4 %all-gather.7.cloned.1.call-done = bf16[8192,128]{1,0:T(8,128)(2,1)} async-done(((bf16[64,128]{1,0:T(8,128)(2,1)}), bf16[8192,128]{1,0:T(8,128)(2,1)}) %all-gather.7.cloned.1.call-update) | async-done | bytes 2097168 | tf_op jit(solution)/shard_map/all_gather | solution.py:75
  271.5 69.5 %while.31 = (s32[]{:T(128)}, f32[4,128]{1,0:T(4,128)S(1)}, f32[4,128]{1,0:T(4,128)S(1)}, f32[4,128,128]{2,1,0:T(8,128)S(1)}, s32[128]{0:T(128)S(1)}, /*index=5*/...) while((s32[]{:T(128)}, f32[4,128]{1,0:T(4,128)S(1)}, ...), condition=%wide.region_3.4_spmd.clone, body=%wide.region_0.3_spmd.clone.sunk | while | flops 136907520 | bytes 4365283 | solution.py:53
  274.4 1.4 convolution_add_fusion.5
  277.3 1.2 fusion.60
  278.8 1.4 convolution_add_fusion.5
  281.6 1.2 fusion.60
  283.1 1.4 convolution_add_fusion.5
  286.0 1.2 fusion.60
  287.4 1.4 convolution_add_fusion.5
  290.3 1.2 fusion.60
  291.8 1.4 convolution_add_fusion.5
  294.7 1.2 fusion.60
  296.1 1.4 convolution_add_fusion.5
  300.5 1.4 convolution_add_fusion.5
  303.4 1.2 fusion.60
  304.8 1.4 convolution_add_fusion.5
  309.2 1.4 convolution_add_fusion.5
  313.5 1.4 convolution_add_fusion.5
  317.9 1.4 convolution_add_fusion.5
  320.7 1.2 fusion.60
  322.2 1.4 convolution_add_fusion.5
  325.1 1.2 fusion.60
  326.5 1.4 convolution_add_fusion.5
  330.9 1.4 convolution_add_fusion.5
  333.8 1.2 fusion.60
  335.2 1.4 convolution_add_fusion.5
  339.6 1.4 convolution_add_fusion.5
  341.0 68.7 %all-gather.11.cloned.1.call-done = bf16[16384,128]{1,0:T(8,128)(2,1)} async-done(((bf16[128,128]{1,0:T(8,128)(2,1)}), bf16[16384,128]{1,0:T(8,128)(2,1)}) %all-gather.11.cloned.1.call-update) | async-done | bytes 4194320 | tf_op jit(solution)/shard_map/all_gather | solution.py:90
  409.7 138.0 %all-gather.9.cloned.1.call-done = bf16[16384,128]{1,0:T(8,128)(2,1)} async-done(((bf16[128,128]{1,0:T(8,128)(2,1)}), bf16[16384,128]{1,0:T(8,128)(2,1)}) %all-gather.9.cloned.1.call-update) | async-done | bytes 4194320 | tf_op jit(solution)/shard_map/all_gather | solution.py:89
  547.7 143.6 %while.30 = (s32[]{:T(128)}, f32[4,128]{1,0:T(4,128)S(1)}, f32[4,128]{1,0:T(4,128)S(1)}, f32[4,128,128]{2,1,0:T(8,128)S(1)}, s32[128]{0:T(128)S(1)}, /*index=5*/...) while((s32[]{:T(128)}, f32[4,128]{1,0:T(4,128)S(1)}, ...), condition=%wide.region_7.8_spmd.clone, body=%wide.region_4.7_spmd.clone.sunk | while | flops 136905856 | bytes 4372195 | solution.py:53
  550.8 1.4 convolution_add_fusion.4
  555.2 1.4 convolution_add_fusion.4
  559.7 1.4 convolution_add_fusion.4
  564.2 1.4 convolution_add_fusion.4
  568.7 1.4 convolution_add_fusion.4
  573.2 1.4 convolution_add_fusion.4
  577.7 1.4 convolution_add_fusion.4
  582.2 1.4 convolution_add_fusion.4
  586.7 1.4 convolution_add_fusion.4
  591.2 1.4 convolution_add_fusion.4
  595.6 1.4 convolution_add_fusion.4
  600.1 1.4 convolution_add_fusion.4
  604.6 1.4 convolution_add_fusion.4
  609.1 1.4 convolution_add_fusion.4
  613.6 1.4 convolution_add_fusion.4
  618.1 1.4 convolution_add_fusion.4
  622.6 1.4 convolution_add_fusion.4
  627.1 1.4 convolution_add_fusion.4
  631.6 1.4 convolution_add_fusion.4
  636.0 1.4 convolution_add_fusion.4
  640.5 1.4 convolution_add_fusion.4
  645.0 1.4 convolution_add_fusion.4
  649.5 1.4 convolution_add_fusion.4
  654.0 1.4 convolution_add_fusion.4
  658.5 1.4 convolution_add_fusion.4
  663.0 1.4 convolution_add_fusion.4
  667.5 1.4 convolution_add_fusion.4
  671.9 1.4 convolution_add_fusion.4
  676.4 1.4 convolution_add_fusion.4
  680.9 1.4 convolution_add_fusion.4
  685.4 1.4 convolution_add_fusion.4
  689.9 1.4 convolution_add_fusion.4
  (481 shorter events, 108.8 us)
Async XLA Ops:
  6.5 95.4 %copy-start = (s32[512]{0:T(512)S(1)}, s32[512]{0:T(512)}, u32[]{:S(2)}) copy-start(s32[512]{0:T(512)} %param.17) | copy-start | bytes 6148
  6.5 4.8 copy-start.1
  6.5 146.6 %all-gather.5.cloned.1.call-start = ((), (), s32[]{:S(2)}) async-start(), calls=%async_computation | async-start | bytes 2113536 | tf_op jit(solution)/shard_map/all_gather | solution.py:74
  7.3 264.2 %all-gather.7.cloned.1.call-start = ((), (), s32[]{:S(2)}) async-start(), calls=%async_computation.1 | async-start | bytes 2113536 | tf_op jit(solution)/shard_map/all_gather | solution.py:75
  8.0 401.7 %all-gather.11.cloned.1.call-start = ((), (), s32[]{:S(2)}) async-start(), calls=%async_computation.3 | async-start | bytes 4227072 | tf_op jit(solution)/shard_map/all_gather | solution.py:90
  8.7 538.9 %all-gather.9.cloned.1.call-start = ((), (), s32[]{:S(2)}) async-start(), calls=%async_computation.2 | async-start | bytes 4227072 | tf_op jit(solution)/shard_map/all_gather | solution.py:89
Sparse Core Ops, SparseCore 0:
  11.8 131.4 all-gather.4
  147.8 123.5 all-gather.6
  275.9 133.6 all-gather.10
  414.0 133.5 all-gather.8
where the time goes:
time: 702 us; the launch traced here: 699 us
  waiting for transfers between devices  328 us (47%)
  local copies, waits for them, and re-layouts  179 us (25%)
  matrix products  124 us (18%)
  loops' own time  33.3 us (5%)
  other arithmetic  20.7 us (3%)
  between operations  13.2 us (2%)
    all_gather x1, waiting for transfers between devices, body(): key_rows = lax.all_gather(new_pair[0], 'ctx', axis=0, tiled=True)  138 us
    all_gather x1, waiting for transfers between devices, body(): value_rows = lax.all_gather(cache_pair[1], 'ctx', axis=0, tiled=True)  118 us
    gather x1, local copies, waits for them, and re-layouts, body(): key_requests = q_request[key_positions]  90.5 us
    all_gather x1, waiting for transfers between devices, body(): value_rows = lax.all_gather(new_pair[1], 'ctx', axis=0, tiled=True)  68.7 us
    dot_general x48, matrix products, attend(): jnp.einsum('hqk,kd->hqd', weights.astype(jnp.bfloat16), value_rows, prefe...  65.6 us
    dot_general x48, matrix products, attend(): jnp.einsum('qhd,kd->hqk', query_rows, key_rows, preferred_element_type=jn...  58.6 us
    gather x1, local copies, waits for them, and re-layouts, body(): key_requests = block_request[global_rows // BLK]  51.2 us
    another operation x2, loops' own time, sweep_keys(): lax.scan(one_step, carry_state, jnp.arange(key_count // block_width, dtyp...  33.3 us
  transfers between devices with their start and end apart: 4, of which 3 were waited for; matrix products, arithmetic and copies ran while one was open for 29% of the time, Pallas kernels for 0%

commit v1 on v0

v1 whole, which is shorter than its diff:
```python
import functools
import math

import jax
import jax.numpy as jnp
from jax import lax
from jax.experimental import pallas as pl
from jax.experimental.pallas import tpu as pltpu
from jax.sharding import Mesh, PartitionSpec as P

HD = 128
BLK = 16
ROWS = 128
CROWS = 64
HEADS = 4
SRC = 64
NEWK = 32
SLOT = NEWK + BLK
GROUP = 8
CHUNK = 512
NEW0 = SRC * BLK + CHUNK
KEYS = NEW0 + SRC * NEWK + CHUNK
LOW = -1.0e30
SCALE2 = math.log2(math.e) / math.sqrt(HD)
PIECE = HEADS * ROWS
STAT = 16

f32, bf16, i32 = jnp.float32, jnp.bfloat16, jnp.int32
VMEM = pl.BlockSpec(memory_space=pltpu.VMEM)
SMEM = pl.BlockSpec(memory_space=pltpu.SMEM)


def pick(index, values):
    out = values[-1]
    for at in range(len(values) - 2, -1, -1):
        out = jnp.where(index == at, values[at], out)
    return out


def prep_kernel(coord, blocks, requests, lo_ref, hi_ref, code_ref, pos, info):
    xh, y, zh, z0, xl = (coord[i] for i in range(5))
    part = xl * 2 + z0
    req = requests[...]
    starts = [jnp.int32(0)] + [
        jnp.sum(jnp.where(req < r, 1.0, 0.0).astype(f32)).astype(i32) for r in (1, 2, 3)
    ]

    def count(i, carry):
        r = blocks[(xh * SRC + i) * 4 + part]
        return tuple(c + jnp.where(r == k, 1, 0) for k, c in enumerate(carry))

    zero = jnp.int32(0)
    n = lax.fori_loop(0, SRC, count, (zero,) * 4)
    offs = [zero, n[0], n[0] + n[1], n[0] + n[1] + n[2], jnp.int32(SRC)]

    def place(i, carry):
        r = blocks[(xh * SRC + i) * 4 + part]
        pos[i] = pick(r, carry)
        return tuple(c + jnp.where(r == k, 1, 0) for k, c in enumerate(carry))

    lax.fori_loop(0, SRC, place, tuple(offs[:4]))

    lane = lax.broadcasted_iota(i32, (1, ROWS), 1)
    for tb in range(4):
        own = (tb // 2) * SRC + y * 8 + zh * 2 + tb % 2
        row = requests[pl.ds(own, 1), :]
        rowf = row.astype(f32)
        first = jnp.min(rowf).astype(i32)
        last = jnp.max(rowf).astype(i32)
        lo = 2 * pick(row, starts)
        hi = 2 * (own * ROWS + lane) + 1
        lo_ref[tb] = jnp.broadcast_to(lo.astype(f32), (ROWS, ROWS)).T
        hi_ref[tb] = jnp.broadcast_to(hi.astype(f32), (ROWS, ROWS)).T
        clo = pick(first, offs[:4]) * BLK
        chi = pick(last, offs[1:]) * BLK
        cs = (clo >> 7) << 7
        info[tb * 4 + 0] = cs
        info[tb * 4 + 1] = jnp.where(chi > clo, (chi - cs + CHUNK - 1) // CHUNK, 0)
        base = xh * SRC
        a = jnp.maximum(pick(first, starts) >> 7, base)
        b = jnp.minimum(own, base + SRC - 1)
        ns = (((a - base) * NEWK) >> 7) << 7
        end = (b - base + 1) * NEWK
        info[tb * 4 + 2] = NEW0 + ns
        info[tb * 4 + 3] = jnp.where(a <= b, (end - ns + CHUNK - 1) // CHUNK, 0)

    key = lax.broadcasted_iota(i32, (8, KEYS), 1)
    block = key >> 4
    cached = jnp.where(
        block >= offs[3],
        starts[3],
        jnp.where(block >= offs[2], starts[2], jnp.where(block >= offs[1], starts[1], 0)),
    )
    u = key - NEW0
    fresh = ROWS * (xh * SRC + (u >> 5)) + NEWK * part + (u & (NEWK - 1))
    code = jnp.where(key < SRC * BLK, 2 * cached, -1)
    code = jnp.where((u >= 0) & (u < SRC * NEWK), 2 * fresh + 1, code)
    code_ref[...] = code.astype(f32)


def attend_kernel(
    coord, pos, info, q_ref, own_ref, got_ref, lo_ref, hi_ref, code_ref, o_ref,
    kbuf, vbuf, qs, m_s, l_s, acc,
):
    for buf in (kbuf, vbuf):
        buf[pl.ds(SRC * BLK, CHUNK), :] = jnp.zeros((CHUNK, HD), bf16)
        buf[pl.ds(KEYS - CHUNK, CHUNK), :] = jnp.zeros((CHUNK, HD), bf16)

    def fill(buf, ref):
        buf[pl.ds(NEW0, SRC * NEWK), :] = ref[:, :NEWK, :].reshape(SRC * NEWK, HD)
        for i in range(SRC):
            to = pl.multiple_of(pos[i] * BLK, BLK)
            buf[pl.ds(to, BLK), :] = ref[i, NEWK:, :]

    @pl.when(coord[5] == 0)
    def _():
        fill(kbuf, own_ref)
        fill(vbuf, got_ref)

    @pl.when(coord[5] == 1)
    def _():
        fill(kbuf, got_ref)
        fill(vbuf, own_ref)

    lane = lax.broadcasted_iota(i32, (ROWS, ROWS), 1)

    def piece_step(piece, unused):
        tb = (piece // 4) * 2 + piece % 2
        for h in range(HEADS):
            qs[pl.ds(h * ROWS, ROWS), :] = q_ref[piece, :, h * HD : (h + 1) * HD]
        m_s[...] = jnp.full(m_s.shape, LOW, f32)
        l_s[...] = jnp.zeros(l_s.shape, f32)
        acc[...] = jnp.zeros(acc.shape, f32)
        cs, nc, ns, nn = (info[tb * 4 + i] for i in range(4))

        def chunk_step(j, unused):
            at = jnp.where(j < nc, cs + j * CHUNK, ns + (j - nc) * CHUNK)
            at = pl.multiple_of(at, 128)
            k = kbuf[pl.ds(at, CHUNK), :]
            v = vbuf[pl.ds(at, CHUNK), :]
            code = code_ref[0:1, pl.ds(at, CHUNK)]
            lo, hi = lo_ref[tb], hi_ref[tb]
            bias = jnp.concatenate(
                [
                    jnp.where((c >= lo) & (c <= hi), 0.0, LOW)
                    for c in (code[:, g * 128 : (g + 1) * 128] for g in range(CHUNK // 128))
                ],
                axis=1,
            )
            s = lax.dot_general(qs[...], k, (((1,), (1,)), ((), ())), preferred_element_type=f32)
            probs, alphas = [], []
            for h in range(HEADS):
                rows = pl.ds(h * ROWS, ROWS)
                sh = s[h * ROWS : (h + 1) * ROWS] + bias
                old = m_s[rows, :]
                new = jnp.maximum(old, jnp.max(sh, axis=1, keepdims=True))
                p = jnp.exp2((sh - new) * SCALE2)
                alpha = jnp.exp2((old - new) * SCALE2)
                m_s[rows, :] = new
                l_s[rows, :] = l_s[rows, :] * alpha + jnp.sum(p, axis=1, keepdims=True)
                probs.append(p.astype(bf16))
                alphas.append(alpha)
            pv = lax.dot_general(
                jnp.concatenate(probs, axis=0), v, (((1,), (0,)), ((), ())), preferred_element_type=f32
            )
            for h in range(HEADS):
                rows = pl.ds(h * ROWS, ROWS)
                acc[rows, :] = acc[rows, :] * alphas[h] + pv[h * ROWS : (h + 1) * ROWS]
            return unused

        lax.fori_loop(0, nc + nn, chunk_step, 0)
        stat = jnp.zeros((ROWS, ROWS), f32)
        for h in range(HEADS):
            rows = pl.ds(h * ROWS, ROWS)
            total = l_s[rows, :]
            total = jnp.where(total > 0.0, total, 1.0)
            o_ref[piece, rows, :] = (acc[rows, :] / total).astype(bf16)
            lse = m_s[rows, :] * SCALE2 + jnp.log2(total)
            stat = jnp.where(lane == h, lse, stat)
        stat = stat.T[:HEADS]
        top = stat.astype(bf16)
        rest = stat - top.astype(f32)
        mid = rest.astype(bf16)
        low = (rest - mid.astype(f32)).astype(bf16)
        o_ref[piece, pl.ds(PIECE, STAT), :] = jnp.concatenate(
            [top.astype(f32), mid.astype(f32), low.astype(f32), jnp.zeros((HEADS, ROWS), f32)], axis=0
        ).astype(bf16)
        return unused

    lax.fori_loop(0, GROUP, piece_step, 0)


def combine_kernel(r_ref, out_ref):
    parts = []
    for i in range(GROUP):
        stat = r_ref[i, pl.ds(PIECE, STAT), :].astype(f32)
        parts.append(stat[0:4] + stat[4:8] + stat[8:12])
    best = functools.reduce(jnp.maximum, parts)
    weights = [jnp.exp2(part - best) for part in parts]
    total = functools.reduce(jnp.add, weights)
    inverse = 1.0 / total
    table = jnp.concatenate([w * inverse for w in weights] + [jnp.zeros((96, ROWS), f32)], axis=0).T
    for h in range(HEADS):
        out = jnp.zeros((ROWS, HD), f32)
        for i in range(GROUP):
            at = i * HEADS + h
            out = out + table[:, at : at + 1] * r_ref[i, pl.ds(h * ROWS, ROWS), :].astype(f32)
        out_ref[:, h * HD : (h + 1) * HD] = out.astype(bf16)


def body(queries, new_keys, new_values, cache_keys, cache_values, q_request, block_request):
    axes = ("xh", "y", "zh", "z0", "xl", "core")
    where = [lax.axis_index(a) for a in axes]
    core, xl = where[5], where[4]
    coord = jnp.stack(where + [jnp.int32(0)] * 2).astype(i32)

    new = jnp.where(core == 0, new_keys, new_values).reshape(2, 2, NEWK, HD)
    old = jnp.where(core == 0, cache_keys, cache_values).reshape(2, 2, BLK, HD)
    both = jnp.concatenate([new, old], axis=2)
    both = jnp.where(xl == 0, both[0], both[1])
    slots = jnp.broadcast_to(both[None], (SRC // 2, 2, SLOT, HD)).reshape(SRC, SLOT, HD)
    held = lax.all_to_all(slots, ("y", "zh", "z0"), 0, 0)
    q_all = lax.all_gather(queries, ("xh", "xl", "z0"), axis=0, tiled=False)

    lo, hi, code, pos, info = pl.pallas_call(
        prep_kernel,
        out_shape=(
            jax.ShapeDtypeStruct((4, ROWS, ROWS), f32),
            jax.ShapeDtypeStruct((4, ROWS, ROWS), f32),
            jax.ShapeDtypeStruct((8, KEYS), f32),
            jax.ShapeDtypeStruct((SRC,), i32),
            jax.ShapeDtypeStruct((16,), i32),
        ),
        in_specs=[SMEM, SMEM, VMEM],
        out_specs=(VMEM, VMEM, VMEM, SMEM, SMEM),
        cost_estimate=pl.CostEstimate(flops=1000000, bytes_accessed=800000, transcendentals=0),
        name="prep",
    )(coord, block_request, q_request.reshape(ROWS, ROWS))

    got = lax.ppermute(held, "core", [(0, 1), (1, 0)])
    partial = pl.pallas_call(
        attend_kernel,
        out_shape=jax.ShapeDtypeStruct((GROUP, PIECE + STAT, HD), bf16),
        in_specs=[SMEM, SMEM, SMEM] + [VMEM] * 6,
        out_specs=VMEM,
        scratch_shapes=[
            pltpu.VMEM((KEYS, HD), bf16),
            pltpu.VMEM((KEYS, HD), bf16),
            pltpu.VMEM((PIECE, HD), bf16),
            pltpu.VMEM((PIECE, 1), f32),
            pltpu.VMEM((PIECE, 1), f32),
            pltpu.VMEM((PIECE, HD), f32),
        ],
        compiler_params=pltpu.CompilerParams(vmem_limit_bytes=32 * 1024 * 1024),
        cost_estimate=pl.CostEstimate(flops=4 * 8000000 * HD, bytes_accessed=4000000, transcendentals=8000000),
        name="attend",
    )(coord, pos, info, q_all, held, got, lo, hi, code)

    shared = lax.all_to_all(partial, ("xh", "xl", "z0"), 0, 0)
    return pl.pallas_call(
        combine_kernel,
        out_shape=jax.ShapeDtypeStruct((ROWS, HEADS * HD), bf16),
        in_specs=[VMEM],
        out_specs=VMEM,
        compiler_params=pltpu.CompilerParams(vmem_limit_bytes=16 * 1024 * 1024),
        name="combine",
    )(shared)


def solution(mesh):
    fine = Mesh(mesh.devices.reshape(2, 8, 4, 2, 2, 2), ("xh", "y", "zh", "z0", "xl", "core"))
    ctx, head = ("xh", "y", "zh", "z0"), ("xl", "core")
    return jax.shard_map(
        body,
        mesh=fine,
        in_specs=(P(ctx, head), P(ctx, None), P(ctx, None), P(ctx, None), P(ctx, None), P(), P()),
        out_specs=P(ctx, head),
        check_vma=False,
    )
```

time: 702 us -> 145 us (0.21)
  waiting for transfers between devices: 328 us -> 44 us
  local copies, waits for them, and re-layouts: 179 us -> 7.66 us
  matrix products: 124 us -> 0 us
  loops' own time: 33.3 us -> 0 us
  blocking collectives: 0 us -> 29.6 us
  Pallas kernels: 0 us -> 29.5 us
  other arithmetic: 20.7 us -> 1.5 us
  starting transfers between devices: 0.12 us -> 18.1 us
    all_gather x4 -> x1, waiting for transfers between devices: 325 us -> 21 us  [body(): q_all = lax.all_gather(queries, ('xh', 'xl', 'z0'), axis=0, tiled=False)]
    gather x2 -> x0, local copies, waits for them, and re-layouts: 142 us -> none  [the longest x1 90.5 us: body(): key_requests = q_request[key_positions]]
    dot_general x96 -> x0, matrix products: 124 us -> none  [the longest x48 65.6 us: attend(): jnp.einsum('hqk,kd->hqd', weights.astype(jnp.bfloat16), value_rows, prefe...]
    dynamic_slice x129 -> x0, local copies, waits for them, and re-layouts: 36.5 us -> none  [the longest x48 29.6 us: sweep_keys(): lax.scan(one_step, carry_state, jnp.arange(key_count // block_width, dtyp...]
    another operation x2 -> x0, loops' own time: 33.3 us -> none  [sweep_keys(): lax.scan(one_step, carry_state, jnp.arange(key_count // block_width, dtyp...]
    all_to_all x0 -> x1, blocking collectives: none -> 29.6 us  [body(): shared = lax.all_to_all(partial, ('xh', 'xl', 'z0'), 0, 0)]
    pallas_call x0 -> x3, Pallas kernels: none -> 29.5 us  [the longest x1 24.4 us: body(): pl.pallas_call(attend_kernel, out_shape=jax.ShapeDtypeStruct((GROUP, PIEC...]
    all_to_all x0 -> x1, waiting for transfers between devices: none -> 22.3 us  [body(): held = lax.all_to_all(slots, ('y', 'zh', 'z0'), 0, 0)]
  transfers between devices with their start and end apart: 4 -> 3, of which waited for: 3 -> 2; matrix products, arithmetic and copies ran while one was open for 29% -> 0% of each run, Pallas kernels for 0% -> 3%
where the time goes in v1:
time: 145 us; the launch traced here: 144 us
  waiting for transfers between devices  44 us (30%)
  blocking collectives  29.6 us (20%)
  Pallas kernels  29.5 us (20%)
  starting transfers between devices  18.1 us (12%)
  between operations  13.5 us (9%)
  local copies, waits for them, and re-layouts  7.66 us (5%)
  other arithmetic  1.5 us (1%)
    all_to_all x1, blocking collectives, body(): shared = lax.all_to_all(partial, ('xh', 'xl', 'z0'), 0, 0)  29.6 us
    pallas_call x1, Pallas kernels, body(): pl.pallas_call(attend_kernel, out_shape=jax.ShapeDtypeStruct((GROUP, PIEC...  24.4 us
    all_to_all x1, waiting for transfers between devices, body(): held = lax.all_to_all(slots, ('y', 'zh', 'z0'), 0, 0)  22.3 us
    all_gather x1, waiting for transfers between devices, body(): q_all = lax.all_gather(queries, ('xh', 'xl', 'z0'), axis=0, tiled=False)  21 us
    all_to_all x1, starting transfers between devices, body(): held = lax.all_to_all(slots, ('y', 'zh', 'z0'), 0, 0)  16.2 us
    unnamed x14, local copies, waits for them, and re-layouts  5.92 us
    pallas_call x1, Pallas kernels, body(): pl.pallas_call(prep_kernel, out_shape=(jax.ShapeDtypeStruct((4, ROWS, ROW...  3.64 us
  transfers between devices with their start and end apart: 3, of which 2 were waited for; matrix products, arithmetic and copies ran while one was open for 0% of the time, Pallas kernels for 3%

profile of v1, /device:TPU:56, one launch (start us, length us, event | category | flops | bytes accessed | tf_op | source)
XLA Modules:
  0.0 143.8 jit_solution(14937085342717140617)
XLA Ops:
  6.5 0.7 broadcast_select_fusion.1
  7.3 0.8 broadcast_select_fusion
  8.0 1.0 broadcast_in_dim.9
  9.1 16.2 %all-to-all-start = ((bf16[64,48,128]{2,1,0:T(8,128)(2,1)}), bf16[64,48,128]{2,1,0:T(8,128)(2,1)S(1)}, u32[]{:S(2)}, u32[]{:S(2)}) async-start(bf16[64,48,128]{2,1,0:T(8,128)(2,1)} %bitcast.11), calls=%async_computation | async-start | bytes 1572864 | tf_op jit(solution)/shard_map/all_to_all | solution.py:222
  25.3 0.0 all-gather.3.cloned.1.call-start
  25.3 0.7 all-gather.3.cloned.1.call-update
  26.0 22.3 %all-to-all-done.own_ref = bf16[64,48,128]{2,1,0:T(8,128)(2,1)S(1)} async-done(((bf16[64,48,128]{2,1,0:T(8,128)(2,1)}), bf16[64,48,128]{2,1,0:T(8,128)(2,1)S(1)}, u32[]{:S(2)}, u32[]{:S(2)}) %all-to-all-start) | async-done | bytes 786464 | tf_op jit(solution)/shard_map/all_to_all | solution.py:222
  48.3 1.9 %collective-permute-start = (bf16[64,48,128]{2,1,0:T(8,128)(2,1)S(1)}, bf16[64,48,128]{2,1,0:T(8,128)(2,1)S(1)}, u32[]{:S(2)}, u32[]{:S(2)}) collective-permute-start(bf16[64,48,128]{2,1,0:T(8,128)(2,1)S(1)} %all-to-all-done.own_ref), channel_id=1, source_target_pairs={{0,1},{1,0},{2,3},{3,2},{4,5},{5,4},{6,7},{7,6},{8,9},{9,8},{10,11... | collective-permute-start | bytes 2359304 | tf_op jit(solution)/shard_map/ppermute | solution.py:240
  50.2 0.7 stack.27.coord
  50.9 3.6 %prep.1 = (f32[4,128,128]{2,1,0:T(8,128)}, f32[4,128,128]{2,1,0:T(8,128)}, f32[8,4096]{1,0:T(8,128)}, s32[64]{0:T(128)}, s32[16]{0:T(128)}) custom-call(s32[8]{0:T(128)} %stack.27.coord, s32[512]{0:T(512)} %blocks.1, s32[128,128]{1,0:T(8,128)} %bitcast.15), custom_call_target="tpu_custom_call" | custom-call | flops 1000000 | bytes 800000 | tf_op jit(solution)/shard_map/prep/pallas_call | solution.py:225
  54.6 21.0 %all-gather.3.cloned.1.call-done = bf16[1024,512]{1,0:T(8,128)(2,1)} async-done(((bf16[128,512]{1,0:T(8,128)(2,1)}), bf16[1024,512]{1,0:T(8,128)(2,1)}) %all-gather.3.cloned.1.call-update) | async-done | bytes 1048592 | tf_op jit(solution)/shard_map/all_gather | solution.py:223
  75.6 0.0 collective-permute-done.got_ref
  75.6 0.0 copy-start
  75.6 0.7 copy-done
  76.2 0.0 copy-start.1
  76.3 1.2 copy-done.1
  77.5 0.0 copy-start.2
  77.5 0.9 copy-done.2
  78.4 0.0 copy-start.3
  78.4 0.9 copy-done.3
  79.4 0.0 copy-start.4
  79.4 0.9 copy-done.4
  80.3 0.0 copy-start.5
  80.3 0.6 copy-done.5
  80.9 0.0 copy-start.6
  80.9 0.6 copy-done.6
  81.5 24.4 %attend.1 = bf16[8,528,128]{2,1,0:T(8,128)(2,1)S(1)} custom-call(s32[8]{0:T(128)S(1)} %copy-done, s32[64]{0:T(128)S(1)} %copy-done.5, s32[16]{0:T(128)S(1)} %copy-done.6, bf16[8,128,512]{2,1,0:T(8,128)(2,1)S(1)} %bitcast.13, bf16[64,48,128]{2,1,0:T(8,128)(2,1)S(1)} %all-to-all-done.own_ref, bf16[64,48,128]{2,1,0:T(8,128)(2,1)S(1)} %collective-permute-done.got_ref, ...), custom_call_target="tpu_custom_call" | custom-call | flops 4096000000 | bytes 4000000 | tf_op jit(solution)/shard_map/attend/pallas_call | solution.py:241
  105.9 29.6 %all_to_all.10.r_ref = bf16[8,528,128]{2,1,0:T(8,128)(2,1)S(1)} all-to-all(bf16[8,528,128]{2,1,0:T(8,128)(2,1)S(1)} %attend.1), channel_id=1, replica_groups=mesh['xh'=2,'y'=8,'zh'=4,'z0'=2,'xl'=2,'core'=2] {'xh','xl','z0'}, dimensions={0} | all-to-all | bytes 2162688 | tf_op jit(solution)/shard_map/all_to_all | solution.py:259
  135.4 1.5 %combine.1 = bf16[128,512]{1,0:T(8,128)(2,1)} custom-call(bf16[8,528,128]{2,1,0:T(8,128)(2,1)S(1)} %all_to_all.10.r_ref), custom_call_target="tpu_custom_call" | custom-call | tf_op jit(solution)/shard_map/combine/pallas_call | solution.py:260
  (2 shorter events, 0.0 us)
Async XLA Ops:
  9.1 39.2 %all-to-all-start = ((bf16[64,48,128]{2,1,0:T(8,128)(2,1)}), bf16[64,48,128]{2,1,0:T(8,128)(2,1)S(1)}, u32[]{:S(2)}, u32[]{:S(2)}) async-start(bf16[64,48,128]{2,1,0:T(8,128)(2,1)} %bitcast.11), calls=%async_computation | async-start | bytes 1572864 | tf_op jit(solution)/shard_map/all_to_all | solution.py:222
  25.3 50.3 %all-gather.3.cloned.1.call-start = ((), (), s32[]{:S(2)}) async-start(), calls=%async_computation.2 | async-start | bytes 1179648 | tf_op jit(solution)/shard_map/all_gather | solution.py:223
  48.3 27.2 %collective-permute-start = (bf16[64,48,128]{2,1,0:T(8,128)(2,1)S(1)}, bf16[64,48,128]{2,1,0:T(8,128)(2,1)S(1)}, u32[]{:S(2)}, u32[]{:S(2)}) collective-permute-start(bf16[64,48,128]{2,1,0:T(8,128)(2,1)S(1)} %all-to-all-done.own_ref), channel_id=1, source_target_pairs={{0,1},{1,0},{2,3},{3,2},{4,5},{5,4},{6,7},{7,6},{8,9},{9,8},{10,11... | collective-permute-start | bytes 2359304 | tf_op jit(solution)/shard_map/ppermute | solution.py:240
  75.6 0.7 copy-start
  76.2 1.2 copy-start.1
  77.5 0.9 copy-start.2
  78.4 0.9 copy-start.3
  79.4 0.9 copy-start.4
  80.3 0.6 copy-start.5
  80.9 0.6 copy-start.6
Sparse Core Ops, SparseCore 0:
  28.2 47.3 all-gather.2

commit v2 on v1

v2 whole, which is shorter than its diff:
```python
import functools
import math

import jax
import jax.numpy as jnp
from jax import lax
from jax.experimental import pallas as pl
from jax.experimental.pallas import tpu as pltpu
from jax.sharding import Mesh, PartitionSpec as P

HD = 128
BLK = 16
ROWS = 128
HEADS = 4
SRC = 64
NEWK = 32
OLDK = 16
PER = OLDK // BLK
SLOT = NEWK + OLDK
GROUP = 8
TBS = 4
SUB1, SUB2 = 256, 256
UNITS = 4
CHUNK = 256
NEW0 = SRC * OLDK + CHUNK
KEYS = NEW0 + SRC * NEWK + CHUNK
STEPS = (SRC * OLDK + SRC * NEWK) // CHUNK
LOW = -1.0e30
SCALE2 = math.log2(math.e) / math.sqrt(HD)
PIECE = HEADS * ROWS
STAT = 16
LO0, HI0, CODE0 = 0, TBS * ROWS, 2 * TBS * ROWS
META = CODE0 + (KEYS // 128 + 7) // 8 * 8
BLOCKS = SRC * PER
TB0, CO0, INFO = BLOCKS, BLOCKS + 4 * TBS, BLOCKS + 4 * TBS + 8

f32, bf16, i32 = jnp.float32, jnp.bfloat16, jnp.int32
VMEM = pl.BlockSpec(memory_space=pltpu.VMEM)
SMEM = pl.BlockSpec(memory_space=pltpu.SMEM)


def pick(index, values):
    out = values[-1]
    for at in range(len(values) - 2, -1, -1):
        out = jnp.where(index == at, values[at], out)
    return out


def prep_kernel(coord, blocks, requests, meta, info):
    xh, y, zh, z0, xl = (coord[i] for i in range(5))
    part = xl * 2 + z0
    for i in range(8):
        info[CO0 + i] = coord[i]
    req = requests[...]
    starts = [jnp.int32(0)] + [
        jnp.sum(jnp.where(req < r, 1.0, 0.0).astype(f32)).astype(i32) for r in (1, 2, 3)
    ]

    def count(i, carry):
        r = blocks[(xh * SRC + i // PER) * 4 + part * PER + i % PER]
        return tuple(c + jnp.where(r == k, 1, 0) for k, c in enumerate(carry))

    zero = jnp.int32(0)
    n = lax.fori_loop(0, BLOCKS, count, (zero,) * 4)
    offs = [zero, n[0], n[0] + n[1], n[0] + n[1] + n[2], jnp.int32(BLOCKS)]

    def place(i, carry):
        r = blocks[(xh * SRC + i // PER) * 4 + part * PER + i % PER]
        info[i] = pick(r, carry)
        return tuple(c + jnp.where(r == k, 1, 0) for k, c in enumerate(carry))

    lax.fori_loop(0, BLOCKS, place, tuple(offs[:4]))

    lane = lax.broadcasted_iota(i32, (1, ROWS), 1)
    for tb in range(TBS):
        own = (tb // 2) * SRC + y * 8 + zh * 2 + tb % 2
        row = requests[pl.ds(own, 1), :]
        rowf = row.astype(f32)
        first = jnp.min(rowf).astype(i32)
        last = jnp.max(rowf).astype(i32)
        lo = 2 * pick(row, starts)
        hi = 2 * (own * ROWS + lane) + 1
        meta[pl.ds(LO0 + tb * ROWS, ROWS), :] = jnp.broadcast_to(lo.astype(f32), (ROWS, ROWS)).T
        meta[pl.ds(HI0 + tb * ROWS, ROWS), :] = jnp.broadcast_to(hi.astype(f32), (ROWS, ROWS)).T
        clo = pick(first, offs[:4]) * BLK
        chi = pick(last, offs[1:]) * BLK
        cs = (clo >> 7) << 7
        info[TB0 + tb * 4 + 0] = cs
        info[TB0 + tb * 4 + 1] = jnp.where(chi > clo, (chi - cs + CHUNK - 1) // CHUNK, 0)
        base = xh * SRC
        a = jnp.maximum(pick(first, starts) >> 7, base)
        b = jnp.minimum(own, base + SRC - 1)
        ns = (((a - base) * NEWK) >> 7) << 7
        end = (b - base + 1) * NEWK
        info[TB0 + tb * 4 + 2] = NEW0 + ns
        info[TB0 + tb * 4 + 3] = jnp.where(a <= b, (end - ns + CHUNK - 1) // CHUNK, 0)

    shape = (META - CODE0, 128)
    key = lax.broadcasted_iota(i32, shape, 0) * 128 + lax.broadcasted_iota(i32, shape, 1)
    block = key >> 4
    cached = jnp.where(
        block >= offs[3],
        starts[3],
        jnp.where(block >= offs[2], starts[2], jnp.where(block >= offs[1], starts[1], 0)),
    )
    u = key - NEW0
    fresh = ROWS * (xh * SRC + (u >> 5)) + NEWK * part + (u & (NEWK - 1))
    code = jnp.where(key < SRC * OLDK, 2 * cached, -1)
    code = jnp.where((u >= 0) & (u < SRC * NEWK), 2 * fresh + 1, code)
    meta[pl.ds(CODE0, META - CODE0), :] = code.astype(f32)


def attend_kernel(info, *refs):
    q_refs, (own_ref, got_ref, meta, o_ref, kbuf, vbuf, qs, ss, mx, sm, acc) = refs[:4], refs[4:]
    for buf in (kbuf, vbuf):
        buf[pl.ds(SRC * OLDK, CHUNK), :] = jnp.zeros((CHUNK, HD), bf16)
        buf[pl.ds(KEYS - CHUNK, CHUNK), :] = jnp.zeros((CHUNK, HD), bf16)

    def fill(buf, ref):
        buf[pl.ds(NEW0, SRC * NEWK), :] = ref[:, :NEWK, :].reshape(SRC * NEWK, HD)
        for i in range(BLOCKS):
            to = pl.multiple_of(info[i] * BLK, BLK)
            buf[pl.ds(to, BLK), :] = ref[i // PER, pl.ds(NEWK + (i % PER) * BLK, BLK), :]

    @pl.when(info[CO0 + 5] == 0)
    def _():
        fill(kbuf, own_ref)
        fill(vbuf, got_ref)

    @pl.when(info[CO0 + 5] == 1)
    def _():
        fill(kbuf, got_ref)
        fill(vbuf, own_ref)

    xh, z0, xl = info[CO0 + 0], info[CO0 + 3], info[CO0 + 4]
    for d in range(4):
        for e in range(2):
            tb = (xh ^ (d >> 1)) * 2 + (z0 ^ e)
            for h in range(HEADS):
                at = pl.multiple_of((xl ^ (d & 1)) * PIECE + h * ROWS, ROWS)
                qs[tb, pl.ds(at, ROWS), :] = q_refs[d][pl.ds(e * ROWS, ROWS), h * HD : (h + 1) * HD]

    lane = lax.broadcasted_iota(i32, (ROWS, ROWS), 1)
    heads = range(2 * HEADS)

    def block_step(tb, unused):
        mx[...] = jnp.full(mx.shape, LOW, f32)
        sm[...] = jnp.zeros(sm.shape, f32)
        acc[...] = jnp.zeros(acc.shape, f32)
        cs, nc, ns, nn = (info[TB0 + tb * 4 + i] for i in range(4))

        def place(j):
            return pl.multiple_of(jnp.where(j < nc, cs + j * CHUNK, ns + (j - nc) * CHUNK), 128)

        def score_step(j, units):
            lo = meta[pl.ds(pl.multiple_of(LO0 + tb * ROWS, ROWS), ROWS), :]
            hi = meta[pl.ds(pl.multiple_of(HI0 + tb * ROWS, ROWS), ROWS), :]
            keys, bias = [], []
            for i in range(units):
                at = place(j + i)
                keys.append(kbuf[pl.ds(at, CHUNK), :])
                for g in range(CHUNK // 128):
                    code = meta[pl.ds(CODE0 + (at >> 7) + g, 1), :]
                    bias.append(jnp.where((code >= lo) & (code <= hi), 0.0, LOW))
            keys = jnp.concatenate(keys, axis=0)
            for h in heads:
                low = h * ROWS % SUB1
                if low == 0:
                    s = lax.dot_general(
                        qs[tb, pl.ds(h * ROWS, SUB1), :], keys, (((1,), (1,)), ((), ())), preferred_element_type=f32
                    )
                rows = pl.ds(h * ROWS, ROWS)
                best = mx[rows, :]
                for g in range(units * CHUNK // 128):
                    part = s[low : low + ROWS, g * 128 : (g + 1) * 128] * SCALE2 + bias[g]
                    ss[j + g // 2, rows, (g % 2) * 128 : (g % 2 + 1) * 128] = part
                    best = jnp.maximum(best, part)
                mx[rows, :] = best

        def sweep(step):
            n = nc + nn

            def most(i, unused):
                step(i * UNITS, UNITS)
                return unused

            lax.fori_loop(0, n // UNITS, most, 0)
            units = UNITS // 2
            while units:
                left = n % (2 * units)

                @pl.when(left >= units)
                def _(units=units, left=left):
                    step(n - left, units)

                units //= 2

        sweep(score_step)
        for h in heads:
            rows = pl.ds(h * ROWS, ROWS)
            mx[rows, :] = jnp.broadcast_to(jnp.max(mx[rows, :], axis=1, keepdims=True), (ROWS, 128))

        def value_step(j, units):
            v = jnp.concatenate([vbuf[pl.ds(place(j + i), CHUNK), :] for i in range(units)], axis=0)
            probs = []
            for h in heads:
                rows = pl.ds(h * ROWS, ROWS)
                best, total = mx[rows, :], sm[rows, :]
                parts = []
                for g in range(units * CHUNK // 128):
                    p = jnp.exp2(ss[j + g // 2, rows, (g % 2) * 128 : (g % 2 + 1) * 128] - best)
                    total = total + p
                    parts.append(p.astype(bf16))
                sm[rows, :] = total
                probs.append(jnp.concatenate(parts, axis=1))
                if len(probs) * ROWS == SUB2:
                    acc[pl.ds((h + 1) * ROWS - SUB2, SUB2), :] += lax.dot_general(
                        jnp.concatenate(probs, axis=0), v, (((1,), (0,)), ((), ())), preferred_element_type=f32
                    )
                    probs = []

        sweep(value_step)
        stat = jnp.zeros((ROWS, ROWS), f32)
        for h in heads:
            rows = pl.ds(h * ROWS, ROWS)
            piece = tb * 2 + h // HEADS
            total = jnp.sum(sm[rows, :], axis=1, keepdims=True)
            total = jnp.where(total > 0.0, total, 1.0)
            o_ref[piece, pl.ds((h % HEADS) * ROWS, ROWS), :] = (acc[rows, :] * (1.0 / total)).astype(bf16)
            lse = mx[rows, 0:1] + jnp.log2(total)
            stat = jnp.where(lane == h, lse, stat)
        stat = stat.T
        for half in range(2):
            piece = tb * 2 + half
            part = stat[half * HEADS : (half + 1) * HEADS]
            top = part.astype(bf16)
            rest = part - top.astype(f32)
            mid = rest.astype(bf16)
            low = (rest - mid.astype(f32)).astype(bf16)
            o_ref[piece, pl.ds(PIECE, STAT), :] = jnp.concatenate(
                [top.astype(f32), mid.astype(f32), low.astype(f32), jnp.zeros((HEADS, ROWS), f32)], axis=0
            ).astype(bf16)
        return unused

    lax.fori_loop(0, TBS, block_step, 0)


def attend(info, queries, held, got, meta):
    return pl.pallas_call(
        attend_kernel,
        out_shape=jax.ShapeDtypeStruct((GROUP, PIECE + STAT, HD), bf16),
        in_specs=[SMEM] + [VMEM] * 7,
        out_specs=VMEM,
        scratch_shapes=[
            pltpu.VMEM((KEYS, HD), bf16),
            pltpu.VMEM((KEYS, HD), bf16),
            pltpu.VMEM((TBS, 2 * PIECE, HD), bf16),
            pltpu.VMEM((STEPS, 2 * PIECE, CHUNK), f32),
            pltpu.VMEM((2 * PIECE, 128), f32),
            pltpu.VMEM((2 * PIECE, 128), f32),
            pltpu.VMEM((2 * PIECE, HD), f32),
        ],
        compiler_params=pltpu.CompilerParams(vmem_limit_bytes=44 * 1024 * 1024),
        cost_estimate=pl.CostEstimate(flops=4 * 8000000 * HD, bytes_accessed=4000000, transcendentals=8000000),
        name="attend",
    )(info, *queries, held, got, meta)


def combine_kernel(r_ref, out_ref):
    parts = []
    for i in range(GROUP):
        stat = r_ref[i, pl.ds(PIECE, STAT), :].astype(f32)
        parts.append(stat[0:4] + stat[4:8] + stat[8:12])
    best = functools.reduce(jnp.maximum, parts)
    weights = [jnp.exp2(part - best) for part in parts]
    total = functools.reduce(jnp.add, weights)
    inverse = 1.0 / total
    table = jnp.concatenate([w * inverse for w in weights] + [jnp.zeros((ROWS - GROUP * HEADS, ROWS), f32)], axis=0).T
    for h in range(HEADS):
        out = jnp.zeros((ROWS, HD), f32)
        for i in range(GROUP):
            at = i * HEADS + h
            out = out + table[:, at : at + 1] * r_ref[i, pl.ds(h * ROWS, ROWS), :].astype(f32)
        out_ref[:, h * HD : (h + 1) * HD] = out.astype(bf16)


def body(queries, new_keys, new_values, cache_keys, cache_values, q_request, block_request):
    axes = ("xh", "y", "zh", "z0", "xl", "core")
    where = [lax.axis_index(a) for a in axes]
    core, xl = where[5], where[4]
    coord = jnp.stack(where + [jnp.int32(0)] * 2).astype(i32)

    across = lax.ppermute(queries, "z0", [(0, 1), (1, 0)])
    new = jnp.where(core == 0, new_keys, new_values).reshape(2, 2, NEWK, HD)
    old = jnp.where(core == 0, cache_keys, cache_values).reshape(2, 2, OLDK, HD)
    both = jnp.concatenate([new, old], axis=2)
    both = jnp.where(xl == 0, both[0], both[1])
    slots = jnp.broadcast_to(both[None], (SRC // 2, 2, SLOT, HD)).reshape(SRC, SLOT, HD)
    slots, across = lax.optimization_barrier((slots, across))
    pair = jnp.concatenate([queries, across], axis=0)
    held = lax.all_to_all(slots, ("y", "zh", "z0"), 0, 0)
    shared = [pair] + [lax.ppermute(pair, ("xh", "xl"), [(i, i ^ d) for i in range(4)]) for d in range(1, 4)]
    meta, info = pl.pallas_call(
        prep_kernel,
        out_shape=(jax.ShapeDtypeStruct((META, 128), f32), jax.ShapeDtypeStruct((INFO,), i32)),
        in_specs=[SMEM, SMEM, VMEM],
        out_specs=(VMEM, SMEM),
        cost_estimate=pl.CostEstimate(flops=1000000, bytes_accessed=800000, transcendentals=0),
        name="prep",
    )(coord, block_request, q_request.reshape(ROWS, ROWS))
    held, meta, info, *shared = lax.optimization_barrier((held, meta, info, *shared))
    got = lax.ppermute(held, "core", [(0, 1), (1, 0)])
    partial = attend(info, shared, held, got, meta)
    parts = lax.all_to_all(partial, ("xh", "z0", "xl"), 0, 0)
    return pl.pallas_call(
        combine_kernel,
        out_shape=jax.ShapeDtypeStruct((ROWS, HEADS * HD), bf16),
        in_specs=[VMEM],
        out_specs=VMEM,
        compiler_params=pltpu.CompilerParams(vmem_limit_bytes=16 * 1024 * 1024),
        name="combine",
    )(parts)


def solution(mesh):
    fine = Mesh(mesh.devices.reshape(2, 8, 4, 2, 2, 2), ("xh", "y", "zh", "z0", "xl", "core"))
    ctx, head = ("xh", "y", "zh", "z0"), ("xl", "core")
    return jax.shard_map(
        body,
        mesh=fine,
        in_specs=(P(ctx, head), P(ctx, None), P(ctx, None), P(ctx, None), P(ctx, None), P(), P()),
        out_specs=P(ctx, head),
        check_vma=False,
    )
```

time: 145 us -> 89.2 us (0.62)
  the two profiles are of different devices: /device:TPU:56 before, /device:TPU:16 now
where the time goes in v2:
time: 89.2 us; the launch traced here: 88.6 us
  starting transfers between devices  31.8 us (36%)
  blocking collectives  19.3 us (22%)
  Pallas kernels  18.2 us (20%)
  waiting for transfers between devices  14.2 us (16%)
  local copies, waits for them, and re-layouts  3.38 us (4%)
  other arithmetic  1.51 us (2%)
    all_to_all x1, blocking collectives, body(): parts = lax.all_to_all(partial, ('xh', 'z0', 'xl'), 0, 0)  19.3 us
    all_to_all x1, starting transfers between devices, body(): held = lax.all_to_all(slots, ('y', 'zh', 'z0'), 0, 0)  15.8 us
    pallas_call x1, Pallas kernels, attend(): pl.pallas_call(attend_kernel, out_shape=jax.ShapeDtypeStruct((GROUP, PIEC...  13 us
    ppermute x3, starting transfers between devices, body(): lax.ppermute(pair, ('xh', 'xl'), [(i, i ^ d) for i in range(4)])  9.82 us
    all_to_all x1, waiting for transfers between devices, body(): held = lax.all_to_all(slots, ('y', 'zh', 'z0'), 0, 0)  6.17 us
    ppermute x1, starting transfers between devices, body(): across = lax.ppermute(queries, 'z0', [(0, 1), (1, 0)])  4.27 us
    pallas_call x1, Pallas kernels, body(): pl.pallas_call(prep_kernel, out_shape=(jax.ShapeDtypeStruct((META, 128),...  3.69 us
    ppermute x3, waiting for transfers between devices, body(): lax.ppermute(pair, ('xh', 'xl'), [(i, i ^ d) for i in range(4)])  3.65 us
  transfers between devices with their start and end apart: 6, of which 6 were waited for; matrix products, arithmetic and copies ran while one was open for 2% of the time, Pallas kernels for 4%

profile of v2, /device:TPU:16, one launch (start us, length us, event | category | flops | bytes accessed | tf_op | source)
XLA Modules:
  0.0 88.6 jit_solution(10140705066383467455)
XLA Ops:
  0.0 4.3 %collective-permute-start = (bf16[128,512]{1,0:T(8,128)(2,1)}, bf16[128,512]{1,0:T(8,128)(2,1)S(1)}, u32[]{:S(2)}, u32[]{:S(2)}) collective-permute-start(bf16[128,512]{1,0:T(8,128)(2,1)} %param.7), channel_id=1, source_target_pairs={{0,4},{4,0},{1,5},{5,1},{2,6},{6,2},{3,7},{7,3},{8,12},{12,8},{9,1... | collective-permute-start | bytes 393224 | tf_op jit(solution)/shard_map/ppermute | solution.py:293
  4.3 0.8 broadcast_select_fusion
  5.1 0.7 broadcast_select_fusion.1
  5.8 0.0 copy-start.2
  5.8 2.2 %collective-permute-done = bf16[128,512]{1,0:T(8,128)(2,1)S(1)} collective-permute-done((bf16[128,512]{1,0:T(8,128)(2,1)}, bf16[128,512]{1,0:T(8,128)(2,1)S(1)}, u32[]{:S(2)}, u32[]{:S(2)}) %collective-permute-start) | collective-permute-done | bytes 131104 | tf_op jit(solution)/shard_map/ppermute | solution.py:293
  8.0 1.0 %broadcast_in_dim.9 = bf16[32,2,48,128]{3,2,1,0:T(8,128)(2,1)} broadcast(bf16[2,48,128]{2,1,0:T(8,128)(2,1)S(1)} %fusion.2), dimensions={1,2,3} | broadcast | bytes 811008 | tf_op jit(solution)/shard_map/broadcast_in_dim | solution.py:298
  8.9 15.8 %all-to-all-start = ((bf16[64,48,128]{2,1,0:T(8,128)(2,1)}), bf16[64,48,128]{2,1,0:T(8,128)(2,1)S(1)}, u32[]{:S(2)}, u32[]{:S(2)}) async-start(bf16[64,48,128]{2,1,0:T(8,128)(2,1)} %bitcast.3), calls=%async_computation | async-start | bytes 1572864 | tf_op jit(solution)/shard_map/all_to_all | solution.py:301
  24.8 0.0 copy-done.2
  24.8 4.7 %collective-permute-start.3 = (bf16[256,512]{1,0:T(8,128)(2,1)S(1)}, bf16[256,512]{1,0:T(8,128)(2,1)S(1)}, u32[]{:S(2)}, u32[]{:S(2)}) collective-permute-start(bf16[256,512]{1,0:T(8,128)(2,1)S(1)} %constant_dynamic-update-slice_fusion.refs_0_), channel_id=1, source_target_pairs={{0,258},{2,256},{256,2},{258,0},{1,259},{3,257},{257,3},{259,1},{4... | collective-permute-start | bytes 786440 | tf_op jit(solution)/shard_map/ppermute | solution.py:302
  29.5 2.7 %collective-permute-start.2 = (bf16[256,512]{1,0:T(8,128)(2,1)S(1)}, bf16[256,512]{1,0:T(8,128)(2,1)S(1)}, u32[]{:S(2)}, u32[]{:S(2)}) collective-permute-start(bf16[256,512]{1,0:T(8,128)(2,1)S(1)} %constant_dynamic-update-slice_fusion.refs_0_), channel_id=1, source_target_pairs={{0,256},{2,258},{256,0},{258,2},{1,257},{3,259},{257,1},{259,3},{4... | collective-permute-start | bytes 786440 | tf_op jit(solution)/shard_map/ppermute | solution.py:302
  32.2 2.4 %collective-permute-start.1 = (bf16[256,512]{1,0:T(8,128)(2,1)S(1)}, bf16[256,512]{1,0:T(8,128)(2,1)S(1)}, u32[]{:S(2)}, u32[]{:S(2)}) collective-permute-start(bf16[256,512]{1,0:T(8,128)(2,1)S(1)} %constant_dynamic-update-slice_fusion.refs_0_), channel_id=1, source_target_pairs={{0,2},{2,0},{256,258},{258,256},{1,3},{3,1},{257,259},{259,257},{4... | collective-permute-start | bytes 786440 | tf_op jit(solution)/shard_map/ppermute | solution.py:302
  34.7 0.7 stack.27.coord
  35.4 3.7 %prep.1 = (f32[1056,128]{1,0:T(8,128)}, s32[88]{0:T(128)}) custom-call(s32[8]{0:T(128)} %stack.27.coord, s32[512]{0:T(512)} %blocks.1, s32[128,128]{1,0:T(8,128)} %bitcast.13), custom_call_target="tpu_custom_call" | custom-call | flops 1000000 | bytes 800000 | tf_op jit(solution)/shard_map/prep/pallas_call | solution.py:303
  39.1 0.2 collective-permute-done.3.refs_3_
  39.3 2.8 %collective-permute-done.2.refs_2_ = bf16[256,512]{1,0:T(8,128)(2,1)S(1)} collective-permute-done((bf16[256,512]{1,0:T(8,128)(2,1)S(1)}, bf16[256,512]{1,0:T(8,128)(2,1)S(1)}, u32[]{:S(2)}, u32[]{:S(2)}) %collective-permute-start.2) | collective-permute-done | bytes 262176 | tf_op jit(solution)/shard_map/ppermute | solution.py:302
  42.1 0.6 collective-permute-done.1.refs_1_
  42.7 6.2 %all-to-all-done.refs_4_ = bf16[64,48,128]{2,1,0:T(8,128)(2,1)S(1)} async-done(((bf16[64,48,128]{2,1,0:T(8,128)(2,1)}), bf16[64,48,128]{2,1,0:T(8,128)(2,1)S(1)}, u32[]{:S(2)}, u32[]{:S(2)}) %all-to-all-start) | async-done | bytes 786464 | tf_op jit(solution)/shard_map/all_to_all | solution.py:301
  48.9 1.9 %collective-permute-start.4 = (bf16[64,48,128]{2,1,0:T(8,128)(2,1)S(1)}, bf16[64,48,128]{2,1,0:T(8,128)(2,1)S(1)}, u32[]{:S(2)}, u32[]{:S(2)}) collective-permute-start(bf16[64,48,128]{2,1,0:T(8,128)(2,1)S(1)} %all-to-all-done.refs_4_), channel_id=1, source_target_pairs={{0,1},{1,0},{2,3},{3,2},{4,5},{5,4},{6,7},{7,6},{8,9},{9,8},{10,11... | collective-permute-start | bytes 2359304 | tf_op jit(solution)/shard_map/ppermute | solution.py:312
  50.8 2.3 %collective-permute-done.4.refs_5_ = bf16[64,48,128]{2,1,0:T(8,128)(2,1)S(1)} collective-permute-done((bf16[64,48,128]{2,1,0:T(8,128)(2,1)S(1)}, bf16[64,48,128]{2,1,0:T(8,128)(2,1)S(1)}, u32[]{:S(2)}, u32[]{:S(2)}) %collective-permute-start.4) | collective-permute-done | bytes 786464 | tf_op jit(solution)/shard_map/ppermute | solution.py:312
  53.1 0.0 copy-start
  53.1 1.0 %copy-done = f32[1056,128]{1,0:T(8,128)S(1)} copy-done((f32[1056,128]{1,0:T(8,128)S(1)}, f32[1056,128]{1,0:T(8,128)}, u32[]{:S(2)}) %copy-start) | copy-done | bytes 540696
  54.1 0.0 copy-start.1
  54.1 0.7 copy-done.1
  54.8 13.0 %attend.1 = bf16[8,528,128]{2,1,0:T(8,128)(2,1)S(1)} custom-call(s32[88]{0:T(128)S(1)} %copy-done.1, bf16[256,512]{1,0:T(8,128)(2,1)S(1)} %constant_dynamic-update-slice_fusion.refs_0_, bf16[256,512]{1,0:T(8,128)(2,1)S(1)} %collective-permute-done.1.refs_1_, bf16[256,512]{1,0:T(8,128)(2,1)S(1)} %collective-permute-done.2.refs_2_, ...), custom_call_target="tpu_custom_call" | custom-call | flops 4096000000 | bytes 4000000 | tf_op jit(solution)/shard_map/attend/pallas_call | solution.py:249
  67.8 19.3 %all_to_all.10.r_ref = bf16[8,528,128]{2,1,0:T(8,128)(2,1)S(1)} all-to-all(bf16[8,528,128]{2,1,0:T(8,128)(2,1)S(1)} %attend.1), channel_id=1, replica_groups=mesh['xh'=2,'y'=8,'zh'=4,'z0'=2,'xl'=2,'core'=2] {'xh','z0','xl'}, dimensions={0} | all-to-all | bytes 2162688 | tf_op jit(solution)/shard_map/all_to_all | solution.py:314
  87.1 1.5 %combine.1 = bf16[128,512]{1,0:T(8,128)(2,1)} custom-call(bf16[8,528,128]{2,1,0:T(8,128)(2,1)S(1)} %all_to_all.10.r_ref), custom_call_target="tpu_custom_call" | custom-call | tf_op jit(solution)/shard_map/combine/pallas_call | solution.py:315
  (4 shorter events, 0.0 us)
Async XLA Ops:
  0.0 8.0 %collective-permute-start = (bf16[128,512]{1,0:T(8,128)(2,1)}, bf16[128,512]{1,0:T(8,128)(2,1)S(1)}, u32[]{:S(2)}, u32[]{:S(2)}) collective-permute-start(bf16[128,512]{1,0:T(8,128)(2,1)} %param.7), channel_id=1, source_target_pairs={{0,4},{4,0},{1,5},{5,1},{2,6},{6,2},{3,7},{7,3},{8,12},{12,8},{9,1... | collective-permute-start | bytes 393224 | tf_op jit(solution)/shard_map/ppermute | solution.py:293
  5.8 19.0 %copy-start.2 = (bf16[128,512]{1,0:T(8,128)(2,1)S(1)}, bf16[128,512]{1,0:T(8,128)(2,1)}, u32[]{:S(2)}) copy-start(bf16[128,512]{1,0:T(8,128)(2,1)} %param.7) | copy-start | bytes 393220
  8.9 39.9 %all-to-all-start = ((bf16[64,48,128]{2,1,0:T(8,128)(2,1)}), bf16[64,48,128]{2,1,0:T(8,128)(2,1)S(1)}, u32[]{:S(2)}, u32[]{:S(2)}) async-start(bf16[64,48,128]{2,1,0:T(8,128)(2,1)} %bitcast.3), calls=%async_computation | async-start | bytes 1572864 | tf_op jit(solution)/shard_map/all_to_all | solution.py:301
  24.8 14.4 %collective-permute-start.3 = (bf16[256,512]{1,0:T(8,128)(2,1)S(1)}, bf16[256,512]{1,0:T(8,128)(2,1)S(1)}, u32[]{:S(2)}, u32[]{:S(2)}) collective-permute-start(bf16[256,512]{1,0:T(8,128)(2,1)S(1)} %constant_dynamic-update-slice_fusion.refs_0_), channel_id=1, source_target_pairs={{0,258},{2,256},{256,2},{258,0},{1,259},{3,257},{257,3},{259,1},{4... | collective-permute-start | bytes 786440 | tf_op jit(solution)/shard_map/ppermute | solution.py:302
  29.5 12.6 %collective-permute-start.2 = (bf16[256,512]{1,0:T(8,128)(2,1)S(1)}, bf16[256,512]{1,0:T(8,128)(2,1)S(1)}, u32[]{:S(2)}, u32[]{:S(2)}) collective-permute-start(bf16[256,512]{1,0:T(8,128)(2,1)S(1)} %constant_dynamic-update-slice_fusion.refs_0_), channel_id=1, source_target_pairs={{0,256},{2,258},{256,0},{258,2},{1,257},{3,259},{257,1},{259,3},{4... | collective-permute-start | bytes 786440 | tf_op jit(solution)/shard_map/ppermute | solution.py:302
  32.2 10.5 %collective-permute-start.1 = (bf16[256,512]{1,0:T(8,128)(2,1)S(1)}, bf16[256,512]{1,0:T(8,128)(2,1)S(1)}, u32[]{:S(2)}, u32[]{:S(2)}) collective-permute-start(bf16[256,512]{1,0:T(8,128)(2,1)S(1)} %constant_dynamic-update-slice_fusion.refs_0_), channel_id=1, source_target_pairs={{0,2},{2,0},{256,258},{258,256},{1,3},{3,1},{257,259},{259,257},{4... | collective-permute-start | bytes 786440 | tf_op jit(solution)/shard_map/ppermute | solution.py:302
  48.9 4.2 %collective-permute-start.4 = (bf16[64,48,128]{2,1,0:T(8,128)(2,1)S(1)}, bf16[64,48,128]{2,1,0:T(8,128)(2,1)S(1)}, u32[]{:S(2)}, u32[]{:S(2)}) collective-permute-start(bf16[64,48,128]{2,1,0:T(8,128)(2,1)S(1)} %all-to-all-done.refs_4_), channel_id=1, source_target_pairs={{0,1},{1,0},{2,3},{3,2},{4,5},{5,4},{6,7},{7,6},{8,9},{9,8},{10,11... | collective-permute-start | bytes 2359304 | tf_op jit(solution)/shard_map/ppermute | solution.py:312
  53.1 1.0 %copy-start = (f32[1056,128]{1,0:T(8,128)S(1)}, f32[1056,128]{1,0:T(8,128)}, u32[]{:S(2)}) copy-start(f32[1056,128]{1,0:T(8,128)} %get-tuple-element.26.refs_6_) | copy-start | bytes 1622020
  54.1 0.7 copy-start.1

commit v3 on v2

--- a/solution.py
+++ b/solution.py
@@ -19,6 +19,7 @@
 SLOT = NEWK + OLDK
 GROUP = 8
 TBS = 4
+PAIRS = TBS // 2
 SUB1, SUB2 = 256, 256
 UNITS = 4
 CHUNK = 256
@@ -28,15 +29,17 @@
 LOW = -1.0e30
 SCALE2 = math.log2(math.e) / math.sqrt(HD)
 PIECE = HEADS * ROWS
+PROWS = 4 * PIECE
 STAT = 16
 LO0, HI0, CODE0 = 0, TBS * ROWS, 2 * TBS * ROWS
 META = CODE0 + (KEYS // 128 + 7) // 8 * 8
 BLOCKS = SRC * PER
-TB0, CO0, INFO = BLOCKS, BLOCKS + 4 * TBS, BLOCKS + 4 * TBS + 8
+TB0, CO0, INFO = BLOCKS, BLOCKS + 4 * PAIRS, BLOCKS + 4 * PAIRS + 8
 
 f32, bf16, i32 = jnp.float32, jnp.bfloat16, jnp.int32
 VMEM = pl.BlockSpec(memory_space=pltpu.VMEM)
 SMEM = pl.BlockSpec(memory_space=pltpu.SMEM)
+ANY = pl.BlockSpec(memory_space=pl.ANY)
 
 
 def pick(index, values):
@@ -72,28 +75,31 @@
     lax.fori_loop(0, BLOCKS, place, tuple(offs[:4]))
 
     lane = lax.broadcasted_iota(i32, (1, ROWS), 1)
-    for tb in range(TBS):
-        own = (tb // 2) * SRC + y * 8 + zh * 2 + tb % 2
-        row = requests[pl.ds(own, 1), :]
-        rowf = row.astype(f32)
-        first = jnp.min(rowf).astype(i32)
-        last = jnp.max(rowf).astype(i32)
-        lo = 2 * pick(row, starts)
-        hi = 2 * (own * ROWS + lane) + 1
-        meta[pl.ds(LO0 + tb * ROWS, ROWS), :] = jnp.broadcast_to(lo.astype(f32), (ROWS, ROWS)).T
-        meta[pl.ds(HI0 + tb * ROWS, ROWS), :] = jnp.broadcast_to(hi.astype(f32), (ROWS, ROWS)).T
+    for pair in range(PAIRS):
+        firsts, lasts = [], []
+        for e in range(2):
+            tb, own = pair * 2 + e, pair * SRC + y * 8 + zh * 2 + e
+            row = requests[pl.ds(own, 1), :]
+            rowf = row.astype(f32)
+            firsts.append(jnp.min(rowf).astype(i32))
+            lasts.append(jnp.max(rowf).astype(i32))
+            lo = 2 * pick(row, starts)
+            hi = 2 * (own * ROWS + lane) + 1
+            meta[pl.ds(LO0 + tb * ROWS, ROWS), :] = jnp.broadcast_to(lo.astype(f32), (ROWS, ROWS)).T
+            meta[pl.ds(HI0 + tb * ROWS, ROWS), :] = jnp.broadcast_to(hi.astype(f32), (ROWS, ROWS)).T
+        first, last = firsts[0], lasts[1]
         clo = pick(first, offs[:4]) * BLK
         chi = pick(last, offs[1:]) * BLK
         cs = (clo >> 7) << 7
-        info[TB0 + tb * 4 + 0] = cs
-        info[TB0 + tb * 4 + 1] = jnp.where(chi > clo, (chi - cs + CHUNK - 1) // CHUNK, 0)
+        info[TB0 + pair * 4 + 0] = cs
+        info[TB0 + pair * 4 + 1] = jnp.where(chi > clo, (chi - cs + CHUNK - 1) // CHUNK, 0)
         base = xh * SRC
         a = jnp.maximum(pick(first, starts) >> 7, base)
         b = jnp.minimum(own, base + SRC - 1)
         ns = (((a - base) * NEWK) >> 7) << 7
         end = (b - base + 1) * NEWK
-        info[TB0 + tb * 4 + 2] = NEW0 + ns
-        info[TB0 + tb * 4 + 3] = jnp.where(a <= b, (end - ns + CHUNK - 1) // CHUNK, 0)
+        info[TB0 + pair * 4 + 2] = NEW0 + ns
+        info[TB0 + pair * 4 + 3] = jnp.where(a <= b, (end - ns + CHUNK - 1) // CHUNK, 0)
 
     shape = (META - CODE0, 128)
     key = lax.broadcasted_iota(i32, shape, 0) * 128 + lax.broadcasted_iota(i32, shape, 1)
@@ -110,17 +116,24 @@
     meta[pl.ds(CODE0, META - CODE0), :] = code.astype(f32)
 
 
-def attend_kernel(info, *refs):
-    q_refs, (own_ref, got_ref, meta, o_ref, kbuf, vbuf, qs, ss, mx, sm, acc) = refs[:4], refs[4:]
-    for buf in (kbuf, vbuf):
-        buf[pl.ds(SRC * OLDK, CHUNK), :] = jnp.zeros((CHUNK, HD), bf16)
-        buf[pl.ds(KEYS - CHUNK, CHUNK), :] = jnp.zeros((CHUNK, HD), bf16)
+def attend_kernel(info_in, *refs):
+    q_refs, refs = refs[:4], refs[4:]
+    own_ref, got_ref, meta_in, o_ref, info, meta, sem, kbuf, vbuf, qs, ss, mx, acc = refs
+    copy_info = pltpu.make_async_copy(info_in, info, sem.at[0])
+    copy_meta = pltpu.make_async_copy(meta_in, meta, sem.at[1])
+    copy_info.start()
+    copy_meta.start()
+    for at in (SRC * OLDK, KEYS - CHUNK):
+        kbuf[pl.ds(at, CHUNK), :] = jnp.zeros((CHUNK, HD), bf16)
+        vbuf[pl.ds(at, CHUNK), :HD] = jnp.zeros((CHUNK, HD), bf16)
+    vbuf[:, HD:] = jnp.ones((KEYS, HD), bf16)
+    copy_info.wait()
 
     def fill(buf, ref):
-        buf[pl.ds(NEW0, SRC * NEWK), :] = ref[:, :NEWK, :].reshape(SRC * NEWK, HD)
+        buf[pl.ds(NEW0, SRC * NEWK), :HD] = ref[:, :NEWK, :].reshape(SRC * NEWK, HD)
         for i in range(BLOCKS):
             to = pl.multiple_of(info[i] * BLK, BLK)
-            buf[pl.ds(to, BLK), :] = ref[i // PER, pl.ds(NEWK + (i % PER) * BLK, BLK), :]
+            buf[pl.ds(to, BLK), :HD] = ref[i // PER, pl.ds(NEWK + (i % PER) * BLK, BLK), :]
 
     @pl.when(info[CO0 + 5] == 0)
     def _():
@@ -135,44 +148,45 @@
     xh, z0, xl = info[CO0 + 0], info[CO0 + 3], info[CO0 + 4]
     for d in range(4):
         for e in range(2):
-            tb = (xh ^ (d >> 1)) * 2 + (z0 ^ e)
             for h in range(HEADS):
-                at = pl.multiple_of((xl ^ (d & 1)) * PIECE + h * ROWS, ROWS)
-                qs[tb, pl.ds(at, ROWS), :] = q_refs[d][pl.ds(e * ROWS, ROWS), h * HD : (h + 1) * HD]
+                at = pl.multiple_of(((z0 ^ e) * 2 + (xl ^ (d & 1))) * PIECE + h * ROWS, ROWS)
+                qs[xh ^ (d >> 1), pl.ds(at, ROWS), :] = q_refs[d][pl.ds(e * ROWS, ROWS), h * HD : (h + 1) * HD]
 
     lane = lax.broadcasted_iota(i32, (ROWS, ROWS), 1)
-    heads = range(2 * HEADS)
-
-    def block_step(tb, unused):
+    heads = range(4 * HEADS)
+    copy_meta.wait()
+
+    def pair_step(pair, unused):
         mx[...] = jnp.full(mx.shape, LOW, f32)
-        sm[...] = jnp.zeros(sm.shape, f32)
         acc[...] = jnp.zeros(acc.shape, f32)
-        cs, nc, ns, nn = (info[TB0 + tb * 4 + i] for i in range(4))
+        cs, nc, ns, nn = (info[TB0 + pair * 4 + i] for i in range(4))
 
         def place(j):
             return pl.multiple_of(jnp.where(j < nc, cs + j * CHUNK, ns + (j - nc) * CHUNK), 128)
 
         def score_step(j, units):
-            lo = meta[pl.ds(pl.multiple_of(LO0 + tb * ROWS, ROWS), ROWS), :]
-            hi = meta[pl.ds(pl.multiple_of(HI0 + tb * ROWS, ROWS), ROWS), :]
-            keys, bias = [], []
+            keys, bias = [], ([], [])
             for i in range(units):
                 at = place(j + i)
                 keys.append(kbuf[pl.ds(at, CHUNK), :])
                 for g in range(CHUNK // 128):
                     code = meta[pl.ds(CODE0 + (at >> 7) + g, 1), :]
-                    bias.append(jnp.where((code >= lo) & (code <= hi), 0.0, LOW))
+                    for e in range(2):
+                        line = (pair * 2 + e) * ROWS
+                        lo = meta[pl.ds(pl.multiple_of(LO0 + line, ROWS), ROWS), :]
+                        hi = meta[pl.ds(pl.multiple_of(HI0 + line, ROWS), ROWS), :]
+                        bias[e].append(jnp.where((code >= lo) & (code <= hi), 0.0, LOW))
             keys = jnp.concatenate(keys, axis=0)
             for h in heads:
                 low = h * ROWS % SUB1
                 if low == 0:
                     s = lax.dot_general(
-                        qs[tb, pl.ds(h * ROWS, SUB1), :], keys, (((1,), (1,)), ((), ())), preferred_element_type=f32
+                        qs[pair, pl.ds(h * ROWS, SUB1), :], keys, (((1,), (1,)), ((), ())), preferred_element_type=f32
                     )
                 rows = pl.ds(h * ROWS, ROWS)
                 best = mx[rows, :]
                 for g in range(units * CHUNK // 128):
-                    part = s[low : low + ROWS, g * 128 : (g + 1) * 128] * SCALE2 + bias[g]
+                    part = s[low : low + ROWS, g * 128 : (g + 1) * 128] * SCALE2 + bias[h // 8][g]
                     ss[j + g // 2, rows, (g % 2) * 128 : (g % 2 + 1) * 128] = part
                     best = jnp.maximum(best, part)
                 mx[rows, :] = best
@@ -205,13 +219,11 @@
             probs = []
             for h in heads:
                 rows = pl.ds(h * ROWS, ROWS)
-                best, total = mx[rows, :], sm[rows, :]
+                best = mx[rows, :]
                 parts = []
                 for g in range(units * CHUNK // 128):
                     p = jnp.exp2(ss[j + g // 2, rows, (g % 2) * 128 : (g % 2 + 1) * 128] - best)
-                    total = total + p
                     parts.append(p.astype(bf16))
-                sm[rows, :] = total
                 probs.append(jnp.concatenate(parts, axis=1))
                 if len(probs) * ROWS == SUB2:
                     acc[pl.ds((h + 1) * ROWS - SUB2, SUB2), :] += lax.dot_general(
@@ -223,44 +235,43 @@
         stat = jnp.zeros((ROWS, ROWS), f32)
         for h in heads:
             rows = pl.ds(h * ROWS, ROWS)
-            piece = tb * 2 + h // HEADS
-            total = jnp.sum(sm[rows, :], axis=1, keepdims=True)
+            total = acc[rows, HD:]
             total = jnp.where(total > 0.0, total, 1.0)
-            o_ref[piece, pl.ds((h % HEADS) * ROWS, ROWS), :] = (acc[rows, :] * (1.0 / total)).astype(bf16)
-            lse = mx[rows, 0:1] + jnp.log2(total)
-            stat = jnp.where(lane == h, lse, stat)
+            o_ref[pair * 4 + h // HEADS, pl.ds((h % HEADS) * ROWS, ROWS), :] = (acc[rows, :HD] / total).astype(bf16)
+            stat = jnp.where(lane == h, mx[rows, :] + jnp.log2(total), stat)
         stat = stat.T
-        for half in range(2):
-            piece = tb * 2 + half
-            part = stat[half * HEADS : (half + 1) * HEADS]
+        for i in range(4):
+            part = stat[i * HEADS : (i + 1) * HEADS]
             top = part.astype(bf16)
             rest = part - top.astype(f32)
             mid = rest.astype(bf16)
             low = (rest - mid.astype(f32)).astype(bf16)
-            o_ref[piece, pl.ds(PIECE, STAT), :] = jnp.concatenate(
+            o_ref[pair * 4 + i, pl.ds(PIECE, STAT), :] = jnp.concatenate(
                 [top.astype(f32), mid.astype(f32), low.astype(f32), jnp.zeros((HEADS, ROWS), f32)], axis=0
             ).astype(bf16)
         return unused
 
-    lax.fori_loop(0, TBS, block_step, 0)
+    lax.fori_loop(0, PAIRS, pair_step, 0)
 
 
 def attend(info, queries, held, got, meta):
     return pl.pallas_call(
         attend_kernel,
         out_shape=jax.ShapeDtypeStruct((GROUP, PIECE + STAT, HD), bf16),
-        in_specs=[SMEM] + [VMEM] * 7,
+        in_specs=[ANY] + [VMEM] * 6 + [ANY],
         out_specs=VMEM,
         scratch_shapes=[
+            pltpu.SMEM((INFO,), i32),
+            pltpu.VMEM((META, 128), f32),
+            pltpu.SemaphoreType.DMA((2,)),
             pltpu.VMEM((KEYS, HD), bf16),
-            pltpu.VMEM((KEYS, HD), bf16),
-            pltpu.VMEM((TBS, 2 * PIECE, HD), bf16),
-            pltpu.VMEM((STEPS, 2 * PIECE, CHUNK), f32),
-            pltpu.VMEM((2 * PIECE, 128), f32),
-            pltpu.VMEM((2 * PIECE, 128), f32),
-            pltpu.VMEM((2 * PIECE, HD), f32),
+            pltpu.VMEM((KEYS, 2 * HD), bf16),
+            pltpu.VMEM((PAIRS, PROWS, HD), bf16),
+            pltpu.VMEM((STEPS, PROWS, CHUNK), f32),
+            pltpu.VMEM((PROWS, 128), f32),
+            pltpu.VMEM((PROWS, 2 * HD), f32),
         ],
-        compiler_params=pltpu.CompilerParams(vmem_limit_bytes=44 * 1024 * 1024),
+        compiler_params=pltpu.CompilerParams(vmem_limit_bytes=48 * 1024 * 1024),
         cost_estimate=pl.CostEstimate(flops=4 * 8000000 * HD, bytes_accessed=4000000, transcendentals=8000000),
         name="attend",
     )(info, *queries, held, got, meta)

time: 89.2 us -> 88 us (0.987)
  Pallas kernels: 18.2 us -> 16.6 us
    pallas_call x1, Pallas kernels: 13 us -> 11.5 us  [attend(): pl.pallas_call(attend_kernel, out_shape=jax.ShapeDtypeStruct((GROUP, PIEC...]
  transfers between devices with their start and end apart: 6 -> 6, of which waited for: 6 -> 6; matrix products, arithmetic and copies ran while one was open for 2% -> 3% of each run, Pallas kernels for 4% -> 4%
where the time goes in v3:
time: 88 us; the launch traced here: 87.5 us
  starting transfers between devices  31.8 us (36%)
  blocking collectives  19.8 us (22%)
  Pallas kernels  16.6 us (19%)
  waiting for transfers between devices  14.2 us (16%)
  local copies, waits for them, and re-layouts  3.38 us (4%)
  other arithmetic  1.51 us (2%)
    all_to_all x1, blocking collectives, body(): parts = lax.all_to_all(partial, ('xh', 'z0', 'xl'), 0, 0)  19.8 us
    all_to_all x1, starting transfers between devices, body(): held = lax.all_to_all(slots, ('y', 'zh', 'z0'), 0, 0)  15.8 us
    pallas_call x1, Pallas kernels, attend(): pl.pallas_call(attend_kernel, out_shape=jax.ShapeDtypeStruct((GROUP, PIEC...  11.5 us
    ppermute x3, starting transfers between devices, body(): lax.ppermute(pair, ('xh', 'xl'), [(i, i ^ d) for i in range(4)])  9.82 us
    all_to_all x1, waiting for transfers between devices, body(): held = lax.all_to_all(slots, ('y', 'zh', 'z0'), 0, 0)  6.17 us
    ppermute x1, starting transfers between devices, body(): across = lax.ppermute(queries, 'z0', [(0, 1), (1, 0)])  4.27 us
    pallas_call x1, Pallas kernels, body(): pl.pallas_call(prep_kernel, out_shape=(jax.ShapeDtypeStruct((META, 128),...  3.68 us
    ppermute x3, waiting for transfers between devices, body(): lax.ppermute(pair, ('xh', 'xl'), [(i, i ^ d) for i in range(4)])  3.65 us
  transfers between devices with their start and end apart: 6, of which 6 were waited for; matrix products, arithmetic and copies ran while one was open for 3% of the time, Pallas kernels for 4%

profile of v3, /device:TPU:16, one launch (start us, length us, event | category | flops | bytes accessed | tf_op | source)
XLA Modules:
  0.0 87.5 jit_solution(2663126787382814292)
XLA Ops:
  0.0 4.3 %collective-permute-start = (bf16[128,512]{1,0:T(8,128)(2,1)}, bf16[128,512]{1,0:T(8,128)(2,1)S(1)}, u32[]{:S(2)}, u32[]{:S(2)}) collective-permute-start(bf16[128,512]{1,0:T(8,128)(2,1)} %param.7), channel_id=1, source_target_pairs={{0,4},{4,0},{1,5},{5,1},{2,6},{6,2},{3,7},{7,3},{8,12},{12,8},{9,1... | collective-permute-start | bytes 393224 | tf_op jit(solution)/shard_map/ppermute | solution.py:304
  4.3 0.8 broadcast_select_fusion
  5.1 0.7 broadcast_select_fusion.1
  5.8 0.0 copy-start.2
  5.8 2.2 %collective-permute-done = bf16[128,512]{1,0:T(8,128)(2,1)S(1)} collective-permute-done((bf16[128,512]{1,0:T(8,128)(2,1)}, bf16[128,512]{1,0:T(8,128)(2,1)S(1)}, u32[]{:S(2)}, u32[]{:S(2)}) %collective-permute-start) | collective-permute-done | bytes 131104 | tf_op jit(solution)/shard_map/ppermute | solution.py:304
  8.0 1.0 %broadcast_in_dim.9 = bf16[32,2,48,128]{3,2,1,0:T(8,128)(2,1)} broadcast(bf16[2,48,128]{2,1,0:T(8,128)(2,1)S(1)} %fusion.2), dimensions={1,2,3} | broadcast | bytes 811008 | tf_op jit(solution)/shard_map/broadcast_in_dim | solution.py:309
  8.9 15.8 %all-to-all-start = ((bf16[64,48,128]{2,1,0:T(8,128)(2,1)}), bf16[64,48,128]{2,1,0:T(8,128)(2,1)S(1)}, u32[]{:S(2)}, u32[]{:S(2)}) async-start(bf16[64,48,128]{2,1,0:T(8,128)(2,1)} %bitcast.3), calls=%async_computation | async-start | bytes 1572864 | tf_op jit(solution)/shard_map/all_to_all | solution.py:312
  24.8 0.0 copy-done.2
  24.8 4.7 %collective-permute-start.3 = (bf16[256,512]{1,0:T(8,128)(2,1)S(1)}, bf16[256,512]{1,0:T(8,128)(2,1)S(1)}, u32[]{:S(2)}, u32[]{:S(2)}) collective-permute-start(bf16[256,512]{1,0:T(8,128)(2,1)S(1)} %constant_dynamic-update-slice_fusion.refs_0_), channel_id=1, source_target_pairs={{0,258},{2,256},{256,2},{258,0},{1,259},{3,257},{257,3},{259,1},{4... | collective-permute-start | bytes 786440 | tf_op jit(solution)/shard_map/ppermute | solution.py:313
  29.5 2.7 %collective-permute-start.2 = (bf16[256,512]{1,0:T(8,128)(2,1)S(1)}, bf16[256,512]{1,0:T(8,128)(2,1)S(1)}, u32[]{:S(2)}, u32[]{:S(2)}) collective-permute-start(bf16[256,512]{1,0:T(8,128)(2,1)S(1)} %constant_dynamic-update-slice_fusion.refs_0_), channel_id=1, source_target_pairs={{0,256},{2,258},{256,0},{258,2},{1,257},{3,259},{257,1},{259,3},{4... | collective-permute-start | bytes 786440 | tf_op jit(solution)/shard_map/ppermute | solution.py:313
  32.2 2.4 %collective-permute-start.1 = (bf16[256,512]{1,0:T(8,128)(2,1)S(1)}, bf16[256,512]{1,0:T(8,128)(2,1)S(1)}, u32[]{:S(2)}, u32[]{:S(2)}) collective-permute-start(bf16[256,512]{1,0:T(8,128)(2,1)S(1)} %constant_dynamic-update-slice_fusion.refs_0_), channel_id=1, source_target_pairs={{0,2},{2,0},{256,258},{258,256},{1,3},{3,1},{257,259},{259,257},{4... | collective-permute-start | bytes 786440 | tf_op jit(solution)/shard_map/ppermute | solution.py:313
  34.7 0.7 stack.27.coord
  35.4 3.7 %prep.1 = (f32[1056,128]{1,0:T(8,128)}, s32[80]{0:T(128)}) custom-call(s32[8]{0:T(128)} %stack.27.coord, s32[512]{0:T(512)} %blocks.1, s32[128,128]{1,0:T(8,128)} %bitcast.13), custom_call_target="tpu_custom_call" | custom-call | flops 1000000 | bytes 800000 | tf_op jit(solution)/shard_map/prep/pallas_call | solution.py:314
  39.1 0.2 collective-permute-done.3.refs_3_
  39.3 2.8 %collective-permute-done.2.refs_2_ = bf16[256,512]{1,0:T(8,128)(2,1)S(1)} collective-permute-done((bf16[256,512]{1,0:T(8,128)(2,1)S(1)}, bf16[256,512]{1,0:T(8,128)(2,1)S(1)}, u32[]{:S(2)}, u32[]{:S(2)}) %collective-permute-start.2) | collective-permute-done | bytes 262176 | tf_op jit(solution)/shard_map/ppermute | solution.py:313
  42.1 0.6 collective-permute-done.1.refs_1_
  42.7 6.2 %all-to-all-done.refs_4_ = bf16[64,48,128]{2,1,0:T(8,128)(2,1)S(1)} async-done(((bf16[64,48,128]{2,1,0:T(8,128)(2,1)}), bf16[64,48,128]{2,1,0:T(8,128)(2,1)S(1)}, u32[]{:S(2)}, u32[]{:S(2)}) %all-to-all-start) | async-done | bytes 786464 | tf_op jit(solution)/shard_map/all_to_all | solution.py:312
  48.9 1.9 %collective-permute-start.4 = (bf16[64,48,128]{2,1,0:T(8,128)(2,1)S(1)}, bf16[64,48,128]{2,1,0:T(8,128)(2,1)S(1)}, u32[]{:S(2)}, u32[]{:S(2)}) collective-permute-start(bf16[64,48,128]{2,1,0:T(8,128)(2,1)S(1)} %all-to-all-done.refs_4_), channel_id=1, source_target_pairs={{0,1},{1,0},{2,3},{3,2},{4,5},{5,4},{6,7},{7,6},{8,9},{9,8},{10,11... | collective-permute-start | bytes 2359304 | tf_op jit(solution)/shard_map/ppermute | solution.py:323
  50.8 2.3 %collective-permute-done.4.refs_5_ = bf16[64,48,128]{2,1,0:T(8,128)(2,1)S(1)} collective-permute-done((bf16[64,48,128]{2,1,0:T(8,128)(2,1)S(1)}, bf16[64,48,128]{2,1,0:T(8,128)(2,1)S(1)}, u32[]{:S(2)}, u32[]{:S(2)}) %collective-permute-start.4) | collective-permute-done | bytes 786464 | tf_op jit(solution)/shard_map/ppermute | solution.py:323
  53.1 0.0 copy-start
  53.1 1.0 %copy-done = f32[1056,128]{1,0:T(8,128)S(1)} copy-done((f32[1056,128]{1,0:T(8,128)S(1)}, f32[1056,128]{1,0:T(8,128)}, u32[]{:S(2)}) %copy-start) | copy-done | bytes 540696
  54.1 0.0 copy-start.1
  54.1 0.7 copy-done.1
  54.8 11.5 %attend.1 = bf16[8,528,128]{2,1,0:T(8,128)(2,1)S(1)} custom-call(s32[80]{0:T(128)S(1)} %copy-done.1, bf16[256,512]{1,0:T(8,128)(2,1)S(1)} %constant_dynamic-update-slice_fusion.refs_0_, bf16[256,512]{1,0:T(8,128)(2,1)S(1)} %collective-permute-done.1.refs_1_, bf16[256,512]{1,0:T(8,128)(2,1)S(1)} %collective-permute-done.2.refs_2_, ...), custom_call_target="tpu_custom_call" | custom-call | flops 4096000000 | bytes 4000000 | tf_op jit(solution)/shard_map/attend/pallas_call | solution.py:258
  66.2 19.8 %all_to_all.10.r_ref = bf16[8,528,128]{2,1,0:T(8,128)(2,1)S(1)} all-to-all(bf16[8,528,128]{2,1,0:T(8,128)(2,1)S(1)} %attend.1), channel_id=1, replica_groups=mesh['xh'=2,'y'=8,'zh'=4,'z0'=2,'xl'=2,'core'=2] {'xh','z0','xl'}, dimensions={0} | all-to-all | bytes 2162688 | tf_op jit(solution)/shard_map/all_to_all | solution.py:325
  86.0 1.5 %combine.1 = bf16[128,512]{1,0:T(8,128)(2,1)} custom-call(bf16[8,528,128]{2,1,0:T(8,128)(2,1)S(1)} %all_to_all.10.r_ref), custom_call_target="tpu_custom_call" | custom-call | tf_op jit(solution)/shard_map/combine/pallas_call | solution.py:326
  (4 shorter events, 0.0 us)
Async XLA Ops:
  0.0 8.0 %collective-permute-start = (bf16[128,512]{1,0:T(8,128)(2,1)}, bf16[128,512]{1,0:T(8,128)(2,1)S(1)}, u32[]{:S(2)}, u32[]{:S(2)}) collective-permute-start(bf16[128,512]{1,0:T(8,128)(2,1)} %param.7), channel_id=1, source_target_pairs={{0,4},{4,0},{1,5},{5,1},{2,6},{6,2},{3,7},{7,3},{8,12},{12,8},{9,1... | collective-permute-start | bytes 393224 | tf_op jit(solution)/shard_map/ppermute | solution.py:304
  5.8 19.0 %copy-start.2 = (bf16[128,512]{1,0:T(8,128)(2,1)S(1)}, bf16[128,512]{1,0:T(8,128)(2,1)}, u32[]{:S(2)}) copy-start(bf16[128,512]{1,0:T(8,128)(2,1)} %param.7) | copy-start | bytes 393220
  8.9 39.9 %all-to-all-start = ((bf16[64,48,128]{2,1,0:T(8,128)(2,1)}), bf16[64,48,128]{2,1,0:T(8,128)(2,1)S(1)}, u32[]{:S(2)}, u32[]{:S(2)}) async-start(bf16[64,48,128]{2,1,0:T(8,128)(2,1)} %bitcast.3), calls=%async_computation | async-start | bytes 1572864 | tf_op jit(solution)/shard_map/all_to_all | solution.py:312
  24.8 14.4 %collective-permute-start.3 = (bf16[256,512]{1,0:T(8,128)(2,1)S(1)}, bf16[256,512]{1,0:T(8,128)(2,1)S(1)}, u32[]{:S(2)}, u32[]{:S(2)}) collective-permute-start(bf16[256,512]{1,0:T(8,128)(2,1)S(1)} %constant_dynamic-update-slice_fusion.refs_0_), channel_id=1, source_target_pairs={{0,258},{2,256},{256,2},{258,0},{1,259},{3,257},{257,3},{259,1},{4... | collective-permute-start | bytes 786440 | tf_op jit(solution)/shard_map/ppermute | solution.py:313
  29.5 12.6 %collective-permute-start.2 = (bf16[256,512]{1,0:T(8,128)(2,1)S(1)}, bf16[256,512]{1,0:T(8,128)(2,1)S(1)}, u32[]{:S(2)}, u32[]{:S(2)}) collective-permute-start(bf16[256,512]{1,0:T(8,128)(2,1)S(1)} %constant_dynamic-update-slice_fusion.refs_0_), channel_id=1, source_target_pairs={{0,256},{2,258},{256,0},{258,2},{1,257},{3,259},{257,1},{259,3},{4... | collective-permute-start | bytes 786440 | tf_op jit(solution)/shard_map/ppermute | solution.py:313
  32.2 10.5 %collective-permute-start.1 = (bf16[256,512]{1,0:T(8,128)(2,1)S(1)}, bf16[256,512]{1,0:T(8,128)(2,1)S(1)}, u32[]{:S(2)}, u32[]{:S(2)}) collective-permute-start(bf16[256,512]{1,0:T(8,128)(2,1)S(1)} %constant_dynamic-update-slice_fusion.refs_0_), channel_id=1, source_target_pairs={{0,2},{2,0},{256,258},{258,256},{1,3},{3,1},{257,259},{259,257},{4... | collective-permute-start | bytes 786440 | tf_op jit(solution)/shard_map/ppermute | solution.py:313
  48.9 4.2 %collective-permute-start.4 = (bf16[64,48,128]{2,1,0:T(8,128)(2,1)S(1)}, bf16[64,48,128]{2,1,0:T(8,128)(2,1)S(1)}, u32[]{:S(2)}, u32[]{:S(2)}) collective-permute-start(bf16[64,48,128]{2,1,0:T(8,128)(2,1)S(1)} %all-to-all-done.refs_4_), channel_id=1, source_target_pairs={{0,1},{1,0},{2,3},{3,2},{4,5},{5,4},{6,7},{7,6},{8,9},{9,8},{10,11... | collective-permute-start | bytes 2359304 | tf_op jit(solution)/shard_map/ppermute | solution.py:323
  53.1 1.0 %copy-start = (f32[1056,128]{1,0:T(8,128)S(1)}, f32[1056,128]{1,0:T(8,128)}, u32[]{:S(2)}) copy-start(f32[1056,128]{1,0:T(8,128)} %get-tuple-element.26.refs_6_) | copy-start | bytes 1622020
  54.1 0.7 copy-start.1

commit v4 on v3

--- a/solution.py
+++ b/solution.py
@@ -34,12 +34,12 @@
 LO0, HI0, CODE0 = 0, TBS * ROWS, 2 * TBS * ROWS
 META = CODE0 + (KEYS // 128 + 7) // 8 * 8
 BLOCKS = SRC * PER
-TB0, CO0, INFO = BLOCKS, BLOCKS + 4 * PAIRS, BLOCKS + 4 * PAIRS + 8
+TB0, INFO = BLOCKS, BLOCKS + 4 * PAIRS
 
 f32, bf16, i32 = jnp.float32, jnp.bfloat16, jnp.int32
 VMEM = pl.BlockSpec(memory_space=pltpu.VMEM)
 SMEM = pl.BlockSpec(memory_space=pltpu.SMEM)
-ANY = pl.BlockSpec(memory_space=pl.ANY)
+HBM = pl.BlockSpec(memory_space=pltpu.HBM)
 
 
 def pick(index, values):
@@ -49,11 +49,30 @@
     return out
 
 
-def prep_kernel(coord, blocks, requests, meta, info):
-    xh, y, zh, z0, xl = (coord[i] for i in range(5))
+def slots_kernel(new_keys, new_values, cache_keys, cache_values, slots):
+    xl, core = lax.axis_index("xl"), lax.axis_index("core")
+
+    def write(new, old):
+        for z0 in range(2):
+            part = xl * 2 + z0
+            fresh = new[pl.ds(pl.multiple_of(part * NEWK, NEWK), NEWK), :]
+            cached = old[pl.ds(pl.multiple_of(part * OLDK, OLDK), OLDK), :]
+            for i in range(z0, SRC, 2):
+                slots[i, :NEWK, :] = fresh
+                slots[i, NEWK:, :] = cached
+
+    @pl.when(core == 0)
+    def _():
+        write(new_keys, cache_keys)
+
+    @pl.when(core == 1)
+    def _():
+        write(new_values, cache_values)
+
+
+def prep_kernel(blocks, requests, meta, info):
+    xh, y, zh, z0, xl = (lax.axis_index(a) for a in ("xh", "y", "zh", "z0", "xl"))
     part = xl * 2 + z0
-    for i in range(8):
-        info[CO0 + i] = coord[i]
     req = requests[...]
     starts = [jnp.int32(0)] + [
         jnp.sum(jnp.where(req < r, 1.0, 0.0).astype(f32)).astype(i32) for r in (1, 2, 3)
@@ -127,6 +146,13 @@
         kbuf[pl.ds(at, CHUNK), :] = jnp.zeros((CHUNK, HD), bf16)
         vbuf[pl.ds(at, CHUNK), :HD] = jnp.zeros((CHUNK, HD), bf16)
     vbuf[:, HD:] = jnp.ones((KEYS, HD), bf16)
+    xh, z0, xl, core = (lax.axis_index(a) for a in ("xh", "z0", "xl", "core"))
+    for d in range(4):
+        for e in range(2):
+            for h in range(HEADS):
+                at = pl.multiple_of(((z0 ^ e) * 2 + (xl ^ (d & 1))) * PIECE + h * ROWS, ROWS)
+                qs[xh ^ (d >> 1), pl.ds(at, ROWS), :] = q_refs[d][pl.ds(e * ROWS, ROWS), h * HD : (h + 1) * HD]
+
     copy_info.wait()
 
     def fill(buf, ref):
@@ -135,22 +161,15 @@
             to = pl.multiple_of(info[i] * BLK, BLK)
             buf[pl.ds(to, BLK), :HD] = ref[i // PER, pl.ds(NEWK + (i % PER) * BLK, BLK), :]
 
-    @pl.when(info[CO0 + 5] == 0)
+    @pl.when(core == 0)
     def _():
         fill(kbuf, own_ref)
         fill(vbuf, got_ref)
 
-    @pl.when(info[CO0 + 5] == 1)
+    @pl.when(core == 1)
     def _():
         fill(kbuf, got_ref)
         fill(vbuf, own_ref)
-
-    xh, z0, xl = info[CO0 + 0], info[CO0 + 3], info[CO0 + 4]
-    for d in range(4):
-        for e in range(2):
-            for h in range(HEADS):
-                at = pl.multiple_of(((z0 ^ e) * 2 + (xl ^ (d & 1))) * PIECE + h * ROWS, ROWS)
-                qs[xh ^ (d >> 1), pl.ds(at, ROWS), :] = q_refs[d][pl.ds(e * ROWS, ROWS), h * HD : (h + 1) * HD]
 
     lane = lax.broadcasted_iota(i32, (ROWS, ROWS), 1)
     heads = range(4 * HEADS)
@@ -232,14 +251,17 @@
                     probs = []
 
         sweep(value_step)
-        stat = jnp.zeros((ROWS, ROWS), f32)
+        best, sums = jnp.zeros((ROWS, ROWS), f32), jnp.ones((ROWS, ROWS), f32)
         for h in heads:
             rows = pl.ds(h * ROWS, ROWS)
             total = acc[rows, HD:]
             total = jnp.where(total > 0.0, total, 1.0)
-            o_ref[pair * 4 + h // HEADS, pl.ds((h % HEADS) * ROWS, ROWS), :] = (acc[rows, :HD] / total).astype(bf16)
-            stat = jnp.where(lane == h, mx[rows, :] + jnp.log2(total), stat)
-        stat = stat.T
+            inverse = pl.reciprocal(total, approx=True)
+            inverse = inverse * (2.0 - total * inverse)
+            o_ref[pair * 4 + h // HEADS, pl.ds((h % HEADS) * ROWS, ROWS), :] = (acc[rows, :HD] * inverse).astype(bf16)
+            best = jnp.where(lane == h, mx[rows, :], best)
+            sums = jnp.where(lane == h, total, sums)
+        stat = (best + jnp.log2(sums)).T
         for i in range(4):
             part = stat[i * HEADS : (i + 1) * HEADS]
             top = part.astype(bf16)
@@ -258,7 +280,7 @@
     return pl.pallas_call(
         attend_kernel,
         out_shape=jax.ShapeDtypeStruct((GROUP, PIECE + STAT, HD), bf16),
-        in_specs=[ANY] + [VMEM] * 6 + [ANY],
+        in_specs=[HBM] + [VMEM] * 6 + [HBM],
         out_specs=VMEM,
         scratch_shapes=[
             pltpu.SMEM((INFO,), i32),
@@ -296,17 +318,15 @@
 
 
 def body(queries, new_keys, new_values, cache_keys, cache_values, q_request, block_request):
-    axes = ("xh", "y", "zh", "z0", "xl", "core")
-    where = [lax.axis_index(a) for a in axes]
-    core, xl = where[5], where[4]
-    coord = jnp.stack(where + [jnp.int32(0)] * 2).astype(i32)
-
     across = lax.ppermute(queries, "z0", [(0, 1), (1, 0)])
-    new = jnp.where(core == 0, new_keys, new_values).reshape(2, 2, NEWK, HD)
-    old = jnp.where(core == 0, cache_keys, cache_values).reshape(2, 2, OLDK, HD)
-    both = jnp.concatenate([new, old], axis=2)
-    both = jnp.where(xl == 0, both[0], both[1])
-    slots = jnp.broadcast_to(both[None], (SRC // 2, 2, SLOT, HD)).reshape(SRC, SLOT, HD)
+    slots = pl.pallas_call(
+        slots_kernel,
+        out_shape=jax.ShapeDtypeStruct((SRC, SLOT, HD), bf16),
+        in_specs=[VMEM] * 4,
+        out_specs=VMEM,
+        cost_estimate=pl.CostEstimate(flops=1000000, bytes_accessed=4000000, transcendentals=0),
+        name="slots",
+    )(new_keys, new_values, cache_keys, cache_values)
     slots, across = lax.optimization_barrier((slots, across))
     pair = jnp.concatenate([queries, across], axis=0)
     held = lax.all_to_all(slots, ("y", "zh", "z0"), 0, 0)
@@ -314,11 +334,12 @@
     meta, info = pl.pallas_call(
         prep_kernel,
         out_shape=(jax.ShapeDtypeStruct((META, 128), f32), jax.ShapeDtypeStruct((INFO,), i32)),
-        in_specs=[SMEM, SMEM, VMEM],
+        in_specs=[SMEM, VMEM],
         out_specs=(VMEM, SMEM),
         cost_estimate=pl.CostEstimate(flops=1000000, bytes_accessed=800000, transcendentals=0),
+        compiler_params=pltpu.CompilerParams(vmem_limit_bytes=8 * 1024 * 1024),
         name="prep",
-    )(coord, block_request, q_request.reshape(ROWS, ROWS))
+    )(block_request, q_request.reshape(ROWS, ROWS))
     held, meta, info, *shared = lax.optimization_barrier((held, meta, info, *shared))
     got = lax.ppermute(held, "core", [(0, 1), (1, 0)])
     partial = attend(info, shared, held, got, meta)

time: 88 us -> 83.5 us (0.949)
  the two profiles are of different devices: /device:TPU:16 before, /device:TPU:48 now
where the time goes in v4:
time: 83.5 us; the launch traced here: 83.1 us
  starting transfers between devices  31.7 us (38%)
  blocking collectives  21.4 us (26%)
  Pallas kernels  16.6 us (20%)
  waiting for transfers between devices  13.3 us (16%)
    all_to_all x1, blocking collectives, body(): parts = lax.all_to_all(partial, ('xh', 'z0', 'xl'), 0, 0)  21.4 us
    all_to_all x1, starting transfers between devices, body(): held = lax.all_to_all(slots, ('y', 'zh', 'z0'), 0, 0)  15.6 us
    pallas_call x1, Pallas kernels, attend(): pl.pallas_call(attend_kernel, out_shape=jax.ShapeDtypeStruct((GROUP, PIEC...  10.3 us
    ppermute x3, starting transfers between devices, body(): lax.ppermute(pair, ('xh', 'xl'), [(i, i ^ d) for i in range(4)])  9.82 us
    ppermute x3, waiting for transfers between devices, body(): lax.ppermute(pair, ('xh', 'xl'), [(i, i ^ d) for i in range(4)])  4.91 us
    ppermute x1, starting transfers between devices, body(): across = lax.ppermute(queries, 'z0', [(0, 1), (1, 0)])  4.4 us
    all_to_all x1, waiting for transfers between devices, body(): held = lax.all_to_all(slots, ('y', 'zh', 'z0'), 0, 0)  4.17 us
    pallas_call x1, Pallas kernels, body(): pl.pallas_call(prep_kernel, out_shape=(jax.ShapeDtypeStruct((META, 128),...  3.09 us
  transfers between devices with their start and end apart: 6, of which 6 were waited for; matrix products, arithmetic and copies ran while one was open for 0% of the time, Pallas kernels for 6%

profile of v4, /device:TPU:48, one launch (start us, length us, event | category | flops | bytes accessed | tf_op | source)
XLA Modules:
  0.0 83.1 jit_solution(2849335360002865720)
XLA Ops:
  0.0 0.0 copy-start.2
  0.0 4.4 %collective-permute-start = (bf16[128,512]{1,0:T(8,128)(2,1)}, bf16[128,512]{1,0:T(8,128)(2,1)S(1)}, u32[]{:S(2)}, u32[]{:S(2)}) collective-permute-start(bf16[128,512]{1,0:T(8,128)(2,1)} %param.7), channel_id=1, source_target_pairs={{0,4},{4,0},{1,5},{5,1},{2,6},{6,2},{3,7},{7,3},{8,12},{12,8},{9,1... | collective-permute-start | bytes 393224 | tf_op jit(solution)/shard_map/ppermute | solution.py:321
  4.4 1.8 %slots.1 = bf16[64,48,128]{2,1,0:T(8,128)(2,1)} custom-call(bf16[128,128]{1,0:T(8,128)(2,1)} %new_keys.1, bf16[128,128]{1,0:T(8,128)(2,1)} %new_values.1, bf16[64,128]{1,0:T(8,128)(2,1)} %cache_keys.1, bf16[64,128]{1,0:T(8,128)(2,1)} %cache_values.1), custom_call_target="tpu_custom_call" | custom-call | flops 1000000 | bytes 4000000 | tf_op jit(solution)/shard_map/slots/pallas_call | solution.py:322
  6.2 0.0 copy-start
  6.2 0.0 copy-start.1
  6.2 1.9 %collective-permute-done = bf16[128,512]{1,0:T(8,128)(2,1)S(1)} collective-permute-done((bf16[128,512]{1,0:T(8,128)(2,1)}, bf16[128,512]{1,0:T(8,128)(2,1)S(1)}, u32[]{:S(2)}, u32[]{:S(2)}) %collective-permute-start) | collective-permute-done | bytes 131104 | tf_op jit(solution)/shard_map/ppermute | solution.py:321
  8.1 15.6 %all-to-all-start = ((bf16[64,48,128]{2,1,0:T(8,128)(2,1)}), bf16[64,48,128]{2,1,0:T(8,128)(2,1)S(1)}, u32[]{:S(2)}, u32[]{:S(2)}) async-start(bf16[64,48,128]{2,1,0:T(8,128)(2,1)} %slots.1), calls=%async_computation | async-start | bytes 1572864 | tf_op jit(solution)/shard_map/all_to_all | solution.py:332
  23.7 0.0 copy-done.2
  23.7 4.7 %collective-permute-start.3 = (bf16[256,512]{1,0:T(8,128)(2,1)S(1)}, bf16[256,512]{1,0:T(8,128)(2,1)S(1)}, u32[]{:S(2)}, u32[]{:S(2)}) collective-permute-start(bf16[256,512]{1,0:T(8,128)(2,1)S(1)} %constant_dynamic-update-slice_fusion.refs_0_), channel_id=1, source_target_pairs={{0,258},{2,256},{256,2},{258,0},{1,259},{3,257},{257,3},{259,1},{4... | collective-permute-start | bytes 786440 | tf_op jit(solution)/shard_map/ppermute | solution.py:333
  28.4 2.7 %collective-permute-start.2 = (bf16[256,512]{1,0:T(8,128)(2,1)S(1)}, bf16[256,512]{1,0:T(8,128)(2,1)S(1)}, u32[]{:S(2)}, u32[]{:S(2)}) collective-permute-start(bf16[256,512]{1,0:T(8,128)(2,1)S(1)} %constant_dynamic-update-slice_fusion.refs_0_), channel_id=1, source_target_pairs={{0,256},{2,258},{256,0},{258,2},{1,257},{3,259},{257,1},{259,3},{4... | collective-permute-start | bytes 786440 | tf_op jit(solution)/shard_map/ppermute | solution.py:333
  31.1 2.4 %collective-permute-start.1 = (bf16[256,512]{1,0:T(8,128)(2,1)S(1)}, bf16[256,512]{1,0:T(8,128)(2,1)S(1)}, u32[]{:S(2)}, u32[]{:S(2)}) collective-permute-start(bf16[256,512]{1,0:T(8,128)(2,1)S(1)} %constant_dynamic-update-slice_fusion.refs_0_), channel_id=1, source_target_pairs={{0,2},{2,0},{256,258},{258,256},{1,3},{3,1},{257,259},{259,257},{4... | collective-permute-start | bytes 786440 | tf_op jit(solution)/shard_map/ppermute | solution.py:333
  33.6 0.0 copy-done
  33.6 0.0 copy-done.1
  33.6 3.1 %prep.1 = (f32[1056,128]{1,0:T(8,128)S(1)}, s32[72]{0:T(128)S(1)}) custom-call(s32[512]{0:T(512)S(1)} %copy-done.1, s32[128,128]{1,0:T(8,128)S(1)} %bitcast.1), custom_call_target="tpu_custom_call" | custom-call | flops 1000000 | bytes 800000 | tf_op jit(solution)/shard_map/prep/pallas_call | solution.py:334
  36.7 1.5 %collective-permute-done.3.refs_3_ = bf16[256,512]{1,0:T(8,128)(2,1)S(1)} collective-permute-done((bf16[256,512]{1,0:T(8,128)(2,1)S(1)}, bf16[256,512]{1,0:T(8,128)(2,1)S(1)}, u32[]{:S(2)}, u32[]{:S(2)}) %collective-permute-start.3) | collective-permute-done | bytes 262176 | tf_op jit(solution)/shard_map/ppermute | solution.py:333
  38.2 2.8 %collective-permute-done.2.refs_2_ = bf16[256,512]{1,0:T(8,128)(2,1)S(1)} collective-permute-done((bf16[256,512]{1,0:T(8,128)(2,1)S(1)}, bf16[256,512]{1,0:T(8,128)(2,1)S(1)}, u32[]{:S(2)}, u32[]{:S(2)}) %collective-permute-start.2) | collective-permute-done | bytes 262176 | tf_op jit(solution)/shard_map/ppermute | solution.py:333
  41.0 0.6 collective-permute-done.1.refs_1_
  41.6 4.2 %all-to-all-done.refs_4_ = bf16[64,48,128]{2,1,0:T(8,128)(2,1)S(1)} async-done(((bf16[64,48,128]{2,1,0:T(8,128)(2,1)}), bf16[64,48,128]{2,1,0:T(8,128)(2,1)S(1)}, u32[]{:S(2)}, u32[]{:S(2)}) %all-to-all-start) | async-done | bytes 786464 | tf_op jit(solution)/shard_map/all_to_all | solution.py:332
  45.8 1.9 %collective-permute-start.4 = (bf16[64,48,128]{2,1,0:T(8,128)(2,1)S(1)}, bf16[64,48,128]{2,1,0:T(8,128)(2,1)S(1)}, u32[]{:S(2)}, u32[]{:S(2)}) collective-permute-start(bf16[64,48,128]{2,1,0:T(8,128)(2,1)S(1)} %all-to-all-done.refs_4_), channel_id=1, source_target_pairs={{0,1},{1,0},{2,3},{3,2},{4,5},{5,4},{6,7},{7,6},{8,9},{9,8},{10,11... | collective-permute-start | bytes 2359304 | tf_op jit(solution)/shard_map/ppermute | solution.py:344
  47.7 2.3 %collective-permute-done.4.refs_5_ = bf16[64,48,128]{2,1,0:T(8,128)(2,1)S(1)} collective-permute-done((bf16[64,48,128]{2,1,0:T(8,128)(2,1)S(1)}, bf16[64,48,128]{2,1,0:T(8,128)(2,1)S(1)}, u32[]{:S(2)}, u32[]{:S(2)}) %collective-permute-start.4) | collective-permute-done | bytes 786464 | tf_op jit(solution)/shard_map/ppermute | solution.py:344
  50.0 10.3 %attend.1 = bf16[8,528,128]{2,1,0:T(8,128)(2,1)S(1)} custom-call(s32[72]{0:T(128)S(1)} %get-tuple-element.20.info_in, bf16[256,512]{1,0:T(8,128)(2,1)S(1)} %constant_dynamic-update-slice_fusion.refs_0_, bf16[256,512]{1,0:T(8,128)(2,1)S(1)} %collective-permute-done.1.refs_1_, bf16[256,512]{1,0:T(8,128)(2,1)S(1)} %collective-permute-done.2.refs_2_, ...), custom_call_target="tpu_custom_call" | custom-call | flops 4096000000 | bytes 4000000 | tf_op jit(solution)/shard_map/attend/pallas_call | solution.py:280
  60.2 21.4 %all_to_all.10.r_ref = bf16[8,528,128]{2,1,0:T(8,128)(2,1)S(1)} all-to-all(bf16[8,528,128]{2,1,0:T(8,128)(2,1)S(1)} %attend.1), channel_id=1, replica_groups=mesh['xh'=2,'y'=8,'zh'=4,'z0'=2,'xl'=2,'core'=2] {'xh','z0','xl'}, dimensions={0} | all-to-all | bytes 2162688 | tf_op jit(solution)/shard_map/all_to_all | solution.py:346
  81.6 1.5 %combine.1 = bf16[128,512]{1,0:T(8,128)(2,1)} custom-call(bf16[8,528,128]{2,1,0:T(8,128)(2,1)S(1)} %all_to_all.10.r_ref), custom_call_target="tpu_custom_call" | custom-call | tf_op jit(solution)/shard_map/combine/pallas_call | solution.py:347
  (2 shorter events, 0.0 us)
Async XLA Ops:
  0.0 23.7 %copy-start.2 = (bf16[128,512]{1,0:T(8,128)(2,1)S(1)}, bf16[128,512]{1,0:T(8,128)(2,1)}, u32[]{:S(2)}) copy-start(bf16[128,512]{1,0:T(8,128)(2,1)} %param.7) | copy-start | bytes 393220
  0.0 8.1 %collective-permute-start = (bf16[128,512]{1,0:T(8,128)(2,1)}, bf16[128,512]{1,0:T(8,128)(2,1)S(1)}, u32[]{:S(2)}, u32[]{:S(2)}) collective-permute-start(bf16[128,512]{1,0:T(8,128)(2,1)} %param.7), channel_id=1, source_target_pairs={{0,4},{4,0},{1,5},{5,1},{2,6},{6,2},{3,7},{7,3},{8,12},{12,8},{9,1... | collective-permute-start | bytes 393224 | tf_op jit(solution)/shard_map/ppermute | solution.py:321
  6.2 27.4 %copy-start = (s32[16384]{0:T(1024)S(1)}, s32[16384]{0:T(1024)}, u32[]{:S(2)}) copy-start(s32[16384]{0:T(1024)} %param.12) | copy-start | bytes 196612
  6.2 27.4 %copy-start.1 = (s32[512]{0:T(512)S(1)}, s32[512]{0:T(512)}, u32[]{:S(2)}) copy-start(s32[512]{0:T(512)} %blocks.1) | copy-start | bytes 6148
  8.1 37.7 %all-to-all-start = ((bf16[64,48,128]{2,1,0:T(8,128)(2,1)}), bf16[64,48,128]{2,1,0:T(8,128)(2,1)S(1)}, u32[]{:S(2)}, u32[]{:S(2)}) async-start(bf16[64,48,128]{2,1,0:T(8,128)(2,1)} %slots.1), calls=%async_computation | async-start | bytes 1572864 | tf_op jit(solution)/shard_map/all_to_all | solution.py:332
  23.7 14.4 %collective-permute-start.3 = (bf16[256,512]{1,0:T(8,128)(2,1)S(1)}, bf16[256,512]{1,0:T(8,128)(2,1)S(1)}, u32[]{:S(2)}, u32[]{:S(2)}) collective-permute-start(bf16[256,512]{1,0:T(8,128)(2,1)S(1)} %constant_dynamic-update-slice_fusion.refs_0_), channel_id=1, source_target_pairs={{0,258},{2,256},{256,2},{258,0},{1,259},{3,257},{257,3},{259,1},{4... | collective-permute-start | bytes 786440 | tf_op jit(solution)/shard_map/ppermute | solution.py:333
  28.4 12.6 %collective-permute-start.2 = (bf16[256,512]{1,0:T(8,128)(2,1)S(1)}, bf16[256,512]{1,0:T(8,128)(2,1)S(1)}, u32[]{:S(2)}, u32[]{:S(2)}) collective-permute-start(bf16[256,512]{1,0:T(8,128)(2,1)S(1)} %constant_dynamic-update-slice_fusion.refs_0_), channel_id=1, source_target_pairs={{0,256},{2,258},{256,0},{258,2},{1,257},{3,259},{257,1},{259,3},{4... | collective-permute-start | bytes 786440 | tf_op jit(solution)/shard_map/ppermute | solution.py:333
  31.1 10.5 %collective-permute-start.1 = (bf16[256,512]{1,0:T(8,128)(2,1)S(1)}, bf16[256,512]{1,0:T(8,128)(2,1)S(1)}, u32[]{:S(2)}, u32[]{:S(2)}) collective-permute-start(bf16[256,512]{1,0:T(8,128)(2,1)S(1)} %constant_dynamic-update-slice_fusion.refs_0_), channel_id=1, source_target_pairs={{0,2},{2,0},{256,258},{258,256},{1,3},{3,1},{257,259},{259,257},{4... | collective-permute-start | bytes 786440 | tf_op jit(solution)/shard_map/ppermute | solution.py:333
  45.8 4.2 %collective-permute-start.4 = (bf16[64,48,128]{2,1,0:T(8,128)(2,1)S(1)}, bf16[64,48,128]{2,1,0:T(8,128)(2,1)S(1)}, u32[]{:S(2)}, u32[]{:S(2)}) collective-permute-start(bf16[64,48,128]{2,1,0:T(8,128)(2,1)S(1)} %all-to-all-done.refs_4_), channel_id=1, source_target_pairs={{0,1},{1,0},{2,3},{3,2},{4,5},{5,4},{6,7},{7,6},{8,9},{9,8},{10,11... | collective-permute-start | bytes 2359304 | tf_op jit(solution)/shard_map/ppermute | solution.py:344

commit v5 on v4

--- a/solution.py
+++ b/solution.py
@@ -327,7 +327,6 @@
         cost_estimate=pl.CostEstimate(flops=1000000, bytes_accessed=4000000, transcendentals=0),
         name="slots",
     )(new_keys, new_values, cache_keys, cache_values)
-    slots, across = lax.optimization_barrier((slots, across))
     pair = jnp.concatenate([queries, across], axis=0)
     held = lax.all_to_all(slots, ("y", "zh", "z0"), 0, 0)
     shared = [pair] + [lax.ppermute(pair, ("xh", "xl"), [(i, i ^ d) for i in range(4)]) for d in range(1, 4)]
@@ -336,7 +335,7 @@
         out_shape=(jax.ShapeDtypeStruct((META, 128), f32), jax.ShapeDtypeStruct((INFO,), i32)),
         in_specs=[SMEM, VMEM],
         out_specs=(VMEM, SMEM),
-        cost_estimate=pl.CostEstimate(flops=1000000, bytes_accessed=800000, transcendentals=0),
+        cost_estimate=pl.CostEstimate(flops=30000000000, bytes_accessed=800000, transcendentals=0),
         compiler_params=pltpu.CompilerParams(vmem_limit_bytes=8 * 1024 * 1024),
         name="prep",
     )(block_request, q_request.reshape(ROWS, ROWS))

time: 83.5 us -> 81.5 us (0.976)
  the two profiles are of different devices: /device:TPU:48 before, /device:TPU:56 now
where the time goes in v5:
time: 81.5 us; the launch traced here: 81 us
  starting transfers between devices  31.5 us (39%)
  blocking collectives  22.3 us (27%)
  Pallas kernels  14.9 us (18%)
  waiting for transfers between devices  12.1 us (15%)
    all_to_all x1, blocking collectives, body(): parts = lax.all_to_all(partial, ('xh', 'z0', 'xl'), 0, 0)  22.3 us
    all_to_all x1, starting transfers between devices, body(): held = lax.all_to_all(slots, ('y', 'zh', 'z0'), 0, 0)  15.4 us
    ppermute x3, starting transfers between devices, body(): lax.ppermute(pair, ('xh', 'xl'), [(i, i ^ d) for i in range(4)])  9.82 us
    pallas_call x1, Pallas kernels, attend(): pl.pallas_call(attend_kernel, out_shape=jax.ShapeDtypeStruct((GROUP, PIEC...  8.57 us
    ppermute x3, waiting for transfers between devices, body(): lax.ppermute(pair, ('xh', 'xl'), [(i, i ^ d) for i in range(4)])  5.5 us
    ppermute x1, starting transfers between devices, body(): across = lax.ppermute(queries, 'z0', [(0, 1), (1, 0)])  4.4 us
    all_to_all x1, waiting for transfers between devices, body(): held = lax.all_to_all(slots, ('y', 'zh', 'z0'), 0, 0)  4.39 us
    pallas_call x1, Pallas kernels, body(): pl.pallas_call(prep_kernel, out_shape=(jax.ShapeDtypeStruct((META, 128),...  3.09 us
  transfers between devices with their start and end apart: 6, of which 5 were waited for; matrix products, arithmetic and copies ran while one was open for 0% of the time, Pallas kernels for 6%

profile of v5, /device:TPU:56, one launch (start us, length us, event | category | flops | bytes accessed | tf_op | source)
XLA Modules:
  0.0 81.0 jit_solution(14030405277472551387)
XLA Ops:
  0.0 0.0 copy-start.2
  0.0 4.4 %collective-permute-start = (bf16[128,512]{1,0:T(8,128)(2,1)}, bf16[128,512]{1,0:T(8,128)(2,1)S(1)}, u32[]{:S(2)}, u32[]{:S(2)}) collective-permute-start(bf16[128,512]{1,0:T(8,128)(2,1)} %param.7), channel_id=1, source_target_pairs={{0,4},{4,0},{1,5},{5,1},{2,6},{6,2},{3,7},{7,3},{8,12},{12,8},{9,1... | collective-permute-start | bytes 393224 | tf_op jit(solution)/shard_map/ppermute | solution.py:321
  4.4 1.8 %slots.1 = bf16[64,48,128]{2,1,0:T(8,128)(2,1)} custom-call(bf16[128,128]{1,0:T(8,128)(2,1)} %new_keys.1, bf16[128,128]{1,0:T(8,128)(2,1)} %new_values.1, bf16[64,128]{1,0:T(8,128)(2,1)} %cache_keys.1, bf16[64,128]{1,0:T(8,128)(2,1)} %cache_values.1), custom_call_target="tpu_custom_call" | custom-call | flops 1000000 | bytes 4000000 | tf_op jit(solution)/shard_map/slots/pallas_call | solution.py:322
  6.2 0.0 copy-start
  6.2 0.0 copy-start.1
  6.2 15.4 %all-to-all-start = ((bf16[64,48,128]{2,1,0:T(8,128)(2,1)}), bf16[64,48,128]{2,1,0:T(8,128)(2,1)S(1)}, u32[]{:S(2)}, u32[]{:S(2)}) async-start(bf16[64,48,128]{2,1,0:T(8,128)(2,1)} %slots.1), calls=%async_computation | async-start | bytes 1572864 | tf_op jit(solution)/shard_map/all_to_all | solution.py:331
  21.6 0.0 copy-done.2
  21.6 0.0 collective-permute-done
  21.6 4.7 %collective-permute-start.3 = (bf16[256,512]{1,0:T(8,128)(2,1)S(1)}, bf16[256,512]{1,0:T(8,128)(2,1)S(1)}, u32[]{:S(2)}, u32[]{:S(2)}) collective-permute-start(bf16[256,512]{1,0:T(8,128)(2,1)S(1)} %constant_dynamic-update-slice_fusion.refs_0_), channel_id=1, source_target_pairs={{0,258},{2,256},{256,2},{258,0},{1,259},{3,257},{257,3},{259,1},{4... | collective-permute-start | bytes 786440 | tf_op jit(solution)/shard_map/ppermute | solution.py:332
  26.3 2.7 %collective-permute-start.2 = (bf16[256,512]{1,0:T(8,128)(2,1)S(1)}, bf16[256,512]{1,0:T(8,128)(2,1)S(1)}, u32[]{:S(2)}, u32[]{:S(2)}) collective-permute-start(bf16[256,512]{1,0:T(8,128)(2,1)S(1)} %constant_dynamic-update-slice_fusion.refs_0_), channel_id=1, source_target_pairs={{0,256},{2,258},{256,0},{258,2},{1,257},{3,259},{257,1},{259,3},{4... | collective-permute-start | bytes 786440 | tf_op jit(solution)/shard_map/ppermute | solution.py:332
  29.0 2.4 %collective-permute-start.1 = (bf16[256,512]{1,0:T(8,128)(2,1)S(1)}, bf16[256,512]{1,0:T(8,128)(2,1)S(1)}, u32[]{:S(2)}, u32[]{:S(2)}) collective-permute-start(bf16[256,512]{1,0:T(8,128)(2,1)S(1)} %constant_dynamic-update-slice_fusion.refs_0_), channel_id=1, source_target_pairs={{0,2},{2,0},{256,258},{258,256},{1,3},{3,1},{257,259},{259,257},{4... | collective-permute-start | bytes 786440 | tf_op jit(solution)/shard_map/ppermute | solution.py:332
  31.5 0.0 copy-done
  31.5 0.0 copy-done.1
  31.5 3.1 %prep.1 = (f32[1056,128]{1,0:T(8,128)S(1)}, s32[72]{0:T(128)S(1)}) custom-call(s32[512]{0:T(512)S(1)} %copy-done.1, s32[128,128]{1,0:T(8,128)S(1)} %bitcast.1), custom_call_target="tpu_custom_call" | custom-call | flops 30000001024 | bytes 800000 | tf_op jit(solution)/shard_map/prep/pallas_call | solution.py:333
  34.6 2.1 %collective-permute-done.3.refs_3_ = bf16[256,512]{1,0:T(8,128)(2,1)S(1)} collective-permute-done((bf16[256,512]{1,0:T(8,128)(2,1)S(1)}, bf16[256,512]{1,0:T(8,128)(2,1)S(1)}, u32[]{:S(2)}, u32[]{:S(2)}) %collective-permute-start.3) | collective-permute-done | bytes 262176 | tf_op jit(solution)/shard_map/ppermute | solution.py:332
  36.7 2.3 %collective-permute-done.2.refs_2_ = bf16[256,512]{1,0:T(8,128)(2,1)S(1)} collective-permute-done((bf16[256,512]{1,0:T(8,128)(2,1)S(1)}, bf16[256,512]{1,0:T(8,128)(2,1)S(1)}, u32[]{:S(2)}, u32[]{:S(2)}) %collective-permute-start.2) | collective-permute-done | bytes 262176 | tf_op jit(solution)/shard_map/ppermute | solution.py:332
  38.9 1.1 %collective-permute-done.1.refs_1_ = bf16[256,512]{1,0:T(8,128)(2,1)S(1)} collective-permute-done((bf16[256,512]{1,0:T(8,128)(2,1)S(1)}, bf16[256,512]{1,0:T(8,128)(2,1)S(1)}, u32[]{:S(2)}, u32[]{:S(2)}) %collective-permute-start.1) | collective-permute-done | bytes 262176 | tf_op jit(solution)/shard_map/ppermute | solution.py:332
  40.1 4.4 %all-to-all-done.refs_4_ = bf16[64,48,128]{2,1,0:T(8,128)(2,1)S(1)} async-done(((bf16[64,48,128]{2,1,0:T(8,128)(2,1)}), bf16[64,48,128]{2,1,0:T(8,128)(2,1)S(1)}, u32[]{:S(2)}, u32[]{:S(2)}) %all-to-all-start) | async-done | bytes 786464 | tf_op jit(solution)/shard_map/all_to_all | solution.py:331
  44.5 1.9 %collective-permute-start.4 = (bf16[64,48,128]{2,1,0:T(8,128)(2,1)S(1)}, bf16[64,48,128]{2,1,0:T(8,128)(2,1)S(1)}, u32[]{:S(2)}, u32[]{:S(2)}) collective-permute-start(bf16[64,48,128]{2,1,0:T(8,128)(2,1)S(1)} %all-to-all-done.refs_4_), channel_id=1, source_target_pairs={{0,1},{1,0},{2,3},{3,2},{4,5},{5,4},{6,7},{7,6},{8,9},{9,8},{10,11... | collective-permute-start | bytes 2359304 | tf_op jit(solution)/shard_map/ppermute | solution.py:343
  46.4 2.3 %collective-permute-done.4.refs_5_ = bf16[64,48,128]{2,1,0:T(8,128)(2,1)S(1)} collective-permute-done((bf16[64,48,128]{2,1,0:T(8,128)(2,1)S(1)}, bf16[64,48,128]{2,1,0:T(8,128)(2,1)S(1)}, u32[]{:S(2)}, u32[]{:S(2)}) %collective-permute-start.4) | collective-permute-done | bytes 786464 | tf_op jit(solution)/shard_map/ppermute | solution.py:343
  48.7 8.6 %attend.1 = bf16[8,528,128]{2,1,0:T(8,128)(2,1)S(1)} custom-call(s32[72]{0:T(128)S(1)} %get-tuple-element.16.info_in, bf16[256,512]{1,0:T(8,128)(2,1)S(1)} %constant_dynamic-update-slice_fusion.refs_0_, bf16[256,512]{1,0:T(8,128)(2,1)S(1)} %collective-permute-done.1.refs_1_, bf16[256,512]{1,0:T(8,128)(2,1)S(1)} %collective-permute-done.2.refs_2_, ...), custom_call_target="tpu_custom_call" | custom-call | flops 4096000000 | bytes 4000000 | tf_op jit(solution)/shard_map/attend/pallas_call | solution.py:280
  57.2 22.3 %all_to_all.10.r_ref = bf16[8,528,128]{2,1,0:T(8,128)(2,1)S(1)} all-to-all(bf16[8,528,128]{2,1,0:T(8,128)(2,1)S(1)} %attend.1), channel_id=1, replica_groups=mesh['xh'=2,'y'=8,'zh'=4,'z0'=2,'xl'=2,'core'=2] {'xh','z0','xl'}, dimensions={0} | all-to-all | bytes 2162688 | tf_op jit(solution)/shard_map/all_to_all | solution.py:345
  79.5 1.5 %combine.1 = bf16[128,512]{1,0:T(8,128)(2,1)} custom-call(bf16[8,528,128]{2,1,0:T(8,128)(2,1)S(1)} %all_to_all.10.r_ref), custom_call_target="tpu_custom_call" | custom-call | tf_op jit(solution)/shard_map/combine/pallas_call | solution.py:346
  (2 shorter events, 0.0 us)
Async XLA Ops:
  0.0 21.6 %copy-start.2 = (bf16[128,512]{1,0:T(8,128)(2,1)S(1)}, bf16[128,512]{1,0:T(8,128)(2,1)}, u32[]{:S(2)}) copy-start(bf16[128,512]{1,0:T(8,128)(2,1)} %param.7) | copy-start | bytes 393220
  0.0 21.6 %collective-permute-start = (bf16[128,512]{1,0:T(8,128)(2,1)}, bf16[128,512]{1,0:T(8,128)(2,1)S(1)}, u32[]{:S(2)}, u32[]{:S(2)}) collective-permute-start(bf16[128,512]{1,0:T(8,128)(2,1)} %param.7), channel_id=1, source_target_pairs={{0,4},{4,0},{1,5},{5,1},{2,6},{6,2},{3,7},{7,3},{8,12},{12,8},{9,1... | collective-permute-start | bytes 393224 | tf_op jit(solution)/shard_map/ppermute | solution.py:321
  6.2 25.3 %copy-start = (s32[16384]{0:T(1024)S(1)}, s32[16384]{0:T(1024)}, u32[]{:S(2)}) copy-start(s32[16384]{0:T(1024)} %param.12) | copy-start | bytes 196612
  6.2 25.3 %copy-start.1 = (s32[512]{0:T(512)S(1)}, s32[512]{0:T(512)}, u32[]{:S(2)}) copy-start(s32[512]{0:T(512)} %blocks.1) | copy-start | bytes 6148
  6.2 38.3 %all-to-all-start = ((bf16[64,48,128]{2,1,0:T(8,128)(2,1)}), bf16[64,48,128]{2,1,0:T(8,128)(2,1)S(1)}, u32[]{:S(2)}, u32[]{:S(2)}) async-start(bf16[64,48,128]{2,1,0:T(8,128)(2,1)} %slots.1), calls=%async_computation | async-start | bytes 1572864 | tf_op jit(solution)/shard_map/all_to_all | solution.py:331
  21.6 15.0 %collective-permute-start.3 = (bf16[256,512]{1,0:T(8,128)(2,1)S(1)}, bf16[256,512]{1,0:T(8,128)(2,1)S(1)}, u32[]{:S(2)}, u32[]{:S(2)}) collective-permute-start(bf16[256,512]{1,0:T(8,128)(2,1)S(1)} %constant_dynamic-update-slice_fusion.refs_0_), channel_id=1, source_target_pairs={{0,258},{2,256},{256,2},{258,0},{1,259},{3,257},{257,3},{259,1},{4... | collective-permute-start | bytes 786440 | tf_op jit(solution)/shard_map/ppermute | solution.py:332
  26.3 12.6 %collective-permute-start.2 = (bf16[256,512]{1,0:T(8,128)(2,1)S(1)}, bf16[256,512]{1,0:T(8,128)(2,1)S(1)}, u32[]{:S(2)}, u32[]{:S(2)}) collective-permute-start(bf16[256,512]{1,0:T(8,128)(2,1)S(1)} %constant_dynamic-update-slice_fusion.refs_0_), channel_id=1, source_target_pairs={{0,256},{2,258},{256,0},{258,2},{1,257},{3,259},{257,1},{259,3},{4... | collective-permute-start | bytes 786440 | tf_op jit(solution)/shard_map/ppermute | solution.py:332
  29.0 11.1 %collective-permute-start.1 = (bf16[256,512]{1,0:T(8,128)(2,1)S(1)}, bf16[256,512]{1,0:T(8,128)(2,1)S(1)}, u32[]{:S(2)}, u32[]{:S(2)}) collective-permute-start(bf16[256,512]{1,0:T(8,128)(2,1)S(1)} %constant_dynamic-update-slice_fusion.refs_0_), channel_id=1, source_target_pairs={{0,2},{2,0},{256,258},{258,256},{1,3},{3,1},{257,259},{259,257},{4... | collective-permute-start | bytes 786440 | tf_op jit(solution)/shard_map/ppermute | solution.py:332
  44.5 4.2 %collective-permute-start.4 = (bf16[64,48,128]{2,1,0:T(8,128)(2,1)S(1)}, bf16[64,48,128]{2,1,0:T(8,128)(2,1)S(1)}, u32[]{:S(2)}, u32[]{:S(2)}) collective-permute-start(bf16[64,48,128]{2,1,0:T(8,128)(2,1)S(1)} %all-to-all-done.refs_4_), channel_id=1, source_target_pairs={{0,1},{1,0},{2,3},{3,2},{4,5},{5,4},{6,7},{7,6},{8,9},{9,8},{10,11... | collective-permute-start | bytes 2359304 | tf_op jit(solution)/shard_map/ppermute | solution.py:343

commit v6 on v5

--- a/solution.py
+++ b/solution.py
@@ -258,7 +258,7 @@
             total = jnp.where(total > 0.0, total, 1.0)
             inverse = pl.reciprocal(total, approx=True)
             inverse = inverse * (2.0 - total * inverse)
-            o_ref[pair * 4 + h // HEADS, pl.ds((h % HEADS) * ROWS, ROWS), :] = (acc[rows, :HD] * inverse).astype(bf16)
+            o_ref[h // HEADS * 2 + pair, pl.ds((h % HEADS) * ROWS, ROWS), :] = (acc[rows, :HD] * inverse).astype(bf16)
             best = jnp.where(lane == h, mx[rows, :], best)
             sums = jnp.where(lane == h, total, sums)
         stat = (best + jnp.log2(sums)).T
@@ -268,7 +268,7 @@
             rest = part - top.astype(f32)
             mid = rest.astype(bf16)
             low = (rest - mid.astype(f32)).astype(bf16)
-            o_ref[pair * 4 + i, pl.ds(PIECE, STAT), :] = jnp.concatenate(
+            o_ref[i * 2 + pair, pl.ds(PIECE, STAT), :] = jnp.concatenate(
                 [top.astype(f32), mid.astype(f32), low.astype(f32), jnp.zeros((HEADS, ROWS), f32)], axis=0
             ).astype(bf16)
         return unused
@@ -342,7 +342,7 @@
     held, meta, info, *shared = lax.optimization_barrier((held, meta, info, *shared))
     got = lax.ppermute(held, "core", [(0, 1), (1, 0)])
     partial = attend(info, shared, held, got, meta)
-    parts = lax.all_to_all(partial, ("xh", "z0", "xl"), 0, 0)
+    parts = lax.all_to_all(partial, ("z0", "xl", "xh"), 0, 0)
     return pl.pallas_call(
         combine_kernel,
         out_shape=jax.ShapeDtypeStruct((ROWS, HEADS * HD), bf16),

time: 81.5 us -> 82.2 us (level)
  Pallas kernels: 14.9 us -> 11.4 us
  blocking collectives: 22.3 us -> 25.8 us
    pallas_call x1, Pallas kernels: 8.57 us -> 5.1 us  [attend(): pl.pallas_call(attend_kernel, out_shape=jax.ShapeDtypeStruct((GROUP, PIEC...]
    all_to_all x1, blocking collectives: 22.3 us -> 25.8 us  [body(): parts = lax.all_to_all(partial, ('z0', 'xl', 'xh'), 0, 0)]
where the time goes in v6:
time: 82.2 us; the launch traced here: 81 us
  starting transfers between devices  31.5 us (38%)
  blocking collectives  25.8 us (31%)
  waiting for transfers between devices  12.1 us (15%)
  Pallas kernels  11.4 us (14%)
    all_to_all x1, blocking collectives, body(): parts = lax.all_to_all(partial, ('z0', 'xl', 'xh'), 0, 0)  25.8 us
    all_to_all x1, starting transfers between devices, body(): held = lax.all_to_all(slots, ('y', 'zh', 'z0'), 0, 0)  15.4 us
    ppermute x3, starting transfers between devices, body(): lax.ppermute(pair, ('xh', 'xl'), [(i, i ^ d) for i in range(4)])  9.82 us
    ppermute x3, waiting for transfers between devices, body(): lax.ppermute(pair, ('xh', 'xl'), [(i, i ^ d) for i in range(4)])  5.5 us
    pallas_call x1, Pallas kernels, attend(): pl.pallas_call(attend_kernel, out_shape=jax.ShapeDtypeStruct((GROUP, PIEC...  5.1 us
    ppermute x1, starting transfers between devices, body(): across = lax.ppermute(queries, 'z0', [(0, 1), (1, 0)])  4.4 us
    all_to_all x1, waiting for transfers between devices, body(): held = lax.all_to_all(slots, ('y', 'zh', 'z0'), 0, 0)  4.39 us
    pallas_call x1, Pallas kernels, body(): pl.pallas_call(prep_kernel, out_shape=(jax.ShapeDtypeStruct((META, 128),...  3.09 us
  transfers between devices with their start and end apart: 6, of which 5 were waited for; matrix products, arithmetic and copies ran while one was open for 0% of the time, Pallas kernels for 6%

profile of v6, /device:TPU:56, one launch (start us, length us, event | category | flops | bytes accessed | tf_op | source)
XLA Modules:
  0.0 81.0 jit_solution(7535843358439591721)
XLA Ops:
  0.0 0.0 copy-start.2
  0.0 4.4 %collective-permute-start = (bf16[128,512]{1,0:T(8,128)(2,1)}, bf16[128,512]{1,0:T(8,128)(2,1)S(1)}, u32[]{:S(2)}, u32[]{:S(2)}) collective-permute-start(bf16[128,512]{1,0:T(8,128)(2,1)} %param.7), channel_id=1, source_target_pairs={{0,4},{4,0},{1,5},{5,1},{2,6},{6,2},{3,7},{7,3},{8,12},{12,8},{9,1... | collective-permute-start | bytes 393224 | tf_op jit(solution)/shard_map/ppermute | solution.py:321
  4.4 1.8 %slots.1 = bf16[64,48,128]{2,1,0:T(8,128)(2,1)} custom-call(bf16[128,128]{1,0:T(8,128)(2,1)} %new_keys.1, bf16[128,128]{1,0:T(8,128)(2,1)} %new_values.1, bf16[64,128]{1,0:T(8,128)(2,1)} %cache_keys.1, bf16[64,128]{1,0:T(8,128)(2,1)} %cache_values.1), custom_call_target="tpu_custom_call" | custom-call | flops 1000000 | bytes 4000000 | tf_op jit(solution)/shard_map/slots/pallas_call | solution.py:322
  6.2 0.0 copy-start
  6.2 0.0 copy-start.1
  6.2 15.4 %all-to-all-start = ((bf16[64,48,128]{2,1,0:T(8,128)(2,1)}), bf16[64,48,128]{2,1,0:T(8,128)(2,1)S(1)}, u32[]{:S(2)}, u32[]{:S(2)}) async-start(bf16[64,48,128]{2,1,0:T(8,128)(2,1)} %slots.1), calls=%async_computation | async-start | bytes 1572864 | tf_op jit(solution)/shard_map/all_to_all | solution.py:331
  21.6 0.0 copy-done.2
  21.6 0.0 collective-permute-done
  21.6 4.7 %collective-permute-start.3 = (bf16[256,512]{1,0:T(8,128)(2,1)S(1)}, bf16[256,512]{1,0:T(8,128)(2,1)S(1)}, u32[]{:S(2)}, u32[]{:S(2)}) collective-permute-start(bf16[256,512]{1,0:T(8,128)(2,1)S(1)} %constant_dynamic-update-slice_fusion.refs_0_), channel_id=1, source_target_pairs={{0,258},{2,256},{256,2},{258,0},{1,259},{3,257},{257,3},{259,1},{4... | collective-permute-start | bytes 786440 | tf_op jit(solution)/shard_map/ppermute | solution.py:332
  26.3 2.7 %collective-permute-start.2 = (bf16[256,512]{1,0:T(8,128)(2,1)S(1)}, bf16[256,512]{1,0:T(8,128)(2,1)S(1)}, u32[]{:S(2)}, u32[]{:S(2)}) collective-permute-start(bf16[256,512]{1,0:T(8,128)(2,1)S(1)} %constant_dynamic-update-slice_fusion.refs_0_), channel_id=1, source_target_pairs={{0,256},{2,258},{256,0},{258,2},{1,257},{3,259},{257,1},{259,3},{4... | collective-permute-start | bytes 786440 | tf_op jit(solution)/shard_map/ppermute | solution.py:332
  29.0 2.4 %collective-permute-start.1 = (bf16[256,512]{1,0:T(8,128)(2,1)S(1)}, bf16[256,512]{1,0:T(8,128)(2,1)S(1)}, u32[]{:S(2)}, u32[]{:S(2)}) collective-permute-start(bf16[256,512]{1,0:T(8,128)(2,1)S(1)} %constant_dynamic-update-slice_fusion.refs_0_), channel_id=1, source_target_pairs={{0,2},{2,0},{256,258},{258,256},{1,3},{3,1},{257,259},{259,257},{4... | collective-permute-start | bytes 786440 | tf_op jit(solution)/shard_map/ppermute | solution.py:332
  31.5 0.0 copy-done
  31.5 0.0 copy-done.1
  31.5 3.1 %prep.1 = (f32[1056,128]{1,0:T(8,128)S(1)}, s32[72]{0:T(128)S(1)}) custom-call(s32[512]{0:T(512)S(1)} %copy-done.1, s32[128,128]{1,0:T(8,128)S(1)} %bitcast.1), custom_call_target="tpu_custom_call" | custom-call | flops 30000001024 | bytes 800000 | tf_op jit(solution)/shard_map/prep/pallas_call | solution.py:333
  34.6 2.1 %collective-permute-done.3.refs_3_ = bf16[256,512]{1,0:T(8,128)(2,1)S(1)} collective-permute-done((bf16[256,512]{1,0:T(8,128)(2,1)S(1)}, bf16[256,512]{1,0:T(8,128)(2,1)S(1)}, u32[]{:S(2)}, u32[]{:S(2)}) %collective-permute-start.3) | collective-permute-done | bytes 262176 | tf_op jit(solution)/shard_map/ppermute | solution.py:332
  36.7 2.3 %collective-permute-done.2.refs_2_ = bf16[256,512]{1,0:T(8,128)(2,1)S(1)} collective-permute-done((bf16[256,512]{1,0:T(8,128)(2,1)S(1)}, bf16[256,512]{1,0:T(8,128)(2,1)S(1)}, u32[]{:S(2)}, u32[]{:S(2)}) %collective-permute-start.2) | collective-permute-done | bytes 262176 | tf_op jit(solution)/shard_map/ppermute | solution.py:332
  38.9 1.1 %collective-permute-done.1.refs_1_ = bf16[256,512]{1,0:T(8,128)(2,1)S(1)} collective-permute-done((bf16[256,512]{1,0:T(8,128)(2,1)S(1)}, bf16[256,512]{1,0:T(8,128)(2,1)S(1)}, u32[]{:S(2)}, u32[]{:S(2)}) %collective-permute-start.1) | collective-permute-done | bytes 262176 | tf_op jit(solution)/shard_map/ppermute | solution.py:332
  40.1 4.4 %all-to-all-done.refs_4_ = bf16[64,48,128]{2,1,0:T(8,128)(2,1)S(1)} async-done(((bf16[64,48,128]{2,1,0:T(8,128)(2,1)}), bf16[64,48,128]{2,1,0:T(8,128)(2,1)S(1)}, u32[]{:S(2)}, u32[]{:S(2)}) %all-to-all-start) | async-done | bytes 786464 | tf_op jit(solution)/shard_map/all_to_all | solution.py:331
  44.5 1.9 %collective-permute-start.4 = (bf16[64,48,128]{2,1,0:T(8,128)(2,1)S(1)}, bf16[64,48,128]{2,1,0:T(8,128)(2,1)S(1)}, u32[]{:S(2)}, u32[]{:S(2)}) collective-permute-start(bf16[64,48,128]{2,1,0:T(8,128)(2,1)S(1)} %all-to-all-done.refs_4_), channel_id=1, source_target_pairs={{0,1},{1,0},{2,3},{3,2},{4,5},{5,4},{6,7},{7,6},{8,9},{9,8},{10,11... | collective-permute-start | bytes 2359304 | tf_op jit(solution)/shard_map/ppermute | solution.py:343
  46.4 2.3 %collective-permute-done.4.refs_5_ = bf16[64,48,128]{2,1,0:T(8,128)(2,1)S(1)} collective-permute-done((bf16[64,48,128]{2,1,0:T(8,128)(2,1)S(1)}, bf16[64,48,128]{2,1,0:T(8,128)(2,1)S(1)}, u32[]{:S(2)}, u32[]{:S(2)}) %collective-permute-start.4) | collective-permute-done | bytes 786464 | tf_op jit(solution)/shard_map/ppermute | solution.py:343
  48.7 5.1 %attend.1 = bf16[8,528,128]{2,1,0:T(8,128)(2,1)S(1)} custom-call(s32[72]{0:T(128)S(1)} %get-tuple-element.16.info_in, bf16[256,512]{1,0:T(8,128)(2,1)S(1)} %constant_dynamic-update-slice_fusion.refs_0_, bf16[256,512]{1,0:T(8,128)(2,1)S(1)} %collective-permute-done.1.refs_1_, bf16[256,512]{1,0:T(8,128)(2,1)S(1)} %collective-permute-done.2.refs_2_, ...), custom_call_target="tpu_custom_call" | custom-call | flops 4096000000 | bytes 4000000 | tf_op jit(solution)/shard_map/attend/pallas_call | solution.py:280
  53.8 25.8 %all_to_all.10.r_ref = bf16[8,528,128]{2,1,0:T(8,128)(2,1)S(1)} all-to-all(bf16[8,528,128]{2,1,0:T(8,128)(2,1)S(1)} %attend.1), channel_id=1, replica_groups=mesh['xh'=2,'y'=8,'zh'=4,'z0'=2,'xl'=2,'core'=2] {'z0','xl','xh'}, dimensions={0} | all-to-all | bytes 2162688 | tf_op jit(solution)/shard_map/all_to_all | solution.py:345
  79.5 1.5 %combine.1 = bf16[128,512]{1,0:T(8,128)(2,1)} custom-call(bf16[8,528,128]{2,1,0:T(8,128)(2,1)S(1)} %all_to_all.10.r_ref), custom_call_target="tpu_custom_call" | custom-call | tf_op jit(solution)/shard_map/combine/pallas_call | solution.py:346
  (2 shorter events, 0.0 us)
Async XLA Ops:
  0.0 21.6 %copy-start.2 = (bf16[128,512]{1,0:T(8,128)(2,1)S(1)}, bf16[128,512]{1,0:T(8,128)(2,1)}, u32[]{:S(2)}) copy-start(bf16[128,512]{1,0:T(8,128)(2,1)} %param.7) | copy-start | bytes 393220
  0.0 21.6 %collective-permute-start = (bf16[128,512]{1,0:T(8,128)(2,1)}, bf16[128,512]{1,0:T(8,128)(2,1)S(1)}, u32[]{:S(2)}, u32[]{:S(2)}) collective-permute-start(bf16[128,512]{1,0:T(8,128)(2,1)} %param.7), channel_id=1, source_target_pairs={{0,4},{4,0},{1,5},{5,1},{2,6},{6,2},{3,7},{7,3},{8,12},{12,8},{9,1... | collective-permute-start | bytes 393224 | tf_op jit(solution)/shard_map/ppermute | solution.py:321
  6.2 25.3 %copy-start = (s32[16384]{0:T(1024)S(1)}, s32[16384]{0:T(1024)}, u32[]{:S(2)}) copy-start(s32[16384]{0:T(1024)} %param.12) | copy-start | bytes 196612
  6.2 25.3 %copy-start.1 = (s32[512]{0:T(512)S(1)}, s32[512]{0:T(512)}, u32[]{:S(2)}) copy-start(s32[512]{0:T(512)} %blocks.1) | copy-start | bytes 6148
  6.2 38.3 %all-to-all-start = ((bf16[64,48,128]{2,1,0:T(8,128)(2,1)}), bf16[64,48,128]{2,1,0:T(8,128)(2,1)S(1)}, u32[]{:S(2)}, u32[]{:S(2)}) async-start(bf16[64,48,128]{2,1,0:T(8,128)(2,1)} %slots.1), calls=%async_computation | async-start | bytes 1572864 | tf_op jit(solution)/shard_map/all_to_all | solution.py:331
  21.6 15.0 %collective-permute-start.3 = (bf16[256,512]{1,0:T(8,128)(2,1)S(1)}, bf16[256,512]{1,0:T(8,128)(2,1)S(1)}, u32[]{:S(2)}, u32[]{:S(2)}) collective-permute-start(bf16[256,512]{1,0:T(8,128)(2,1)S(1)} %constant_dynamic-update-slice_fusion.refs_0_), channel_id=1, source_target_pairs={{0,258},{2,256},{256,2},{258,0},{1,259},{3,257},{257,3},{259,1},{4... | collective-permute-start | bytes 786440 | tf_op jit(solution)/shard_map/ppermute | solution.py:332
  26.3 12.6 %collective-permute-start.2 = (bf16[256,512]{1,0:T(8,128)(2,1)S(1)}, bf16[256,512]{1,0:T(8,128)(2,1)S(1)}, u32[]{:S(2)}, u32[]{:S(2)}) collective-permute-start(bf16[256,512]{1,0:T(8,128)(2,1)S(1)} %constant_dynamic-update-slice_fusion.refs_0_), channel_id=1, source_target_pairs={{0,256},{2,258},{256,0},{258,2},{1,257},{3,259},{257,1},{259,3},{4... | collective-permute-start | bytes 786440 | tf_op jit(solution)/shard_map/ppermute | solution.py:332
  29.0 11.1 %collective-permute-start.1 = (bf16[256,512]{1,0:T(8,128)(2,1)S(1)}, bf16[256,512]{1,0:T(8,128)(2,1)S(1)}, u32[]{:S(2)}, u32[]{:S(2)}) collective-permute-start(bf16[256,512]{1,0:T(8,128)(2,1)S(1)} %constant_dynamic-update-slice_fusion.refs_0_), channel_id=1, source_target_pairs={{0,2},{2,0},{256,258},{258,256},{1,3},{3,1},{257,259},{259,257},{4... | collective-permute-start | bytes 786440 | tf_op jit(solution)/shard_map/ppermute | solution.py:332
  44.5 4.2 %collective-permute-start.4 = (bf16[64,48,128]{2,1,0:T(8,128)(2,1)S(1)}, bf16[64,48,128]{2,1,0:T(8,128)(2,1)S(1)}, u32[]{:S(2)}, u32[]{:S(2)}) collective-permute-start(bf16[64,48,128]{2,1,0:T(8,128)(2,1)S(1)} %all-to-all-done.refs_4_), channel_id=1, source_target_pairs={{0,1},{1,0},{2,3},{3,2},{4,5},{5,4},{6,7},{7,6},{8,9},{9,8},{10,11... | collective-permute-start | bytes 2359304 | tf_op jit(solution)/shard_map/ppermute | solution.py:343

commit v7 on v6

--- a/solution.py
+++ b/solution.py
@@ -176,9 +176,13 @@
     copy_meta.wait()
 
     def pair_step(pair, unused):
-        mx[...] = jnp.full(mx.shape, LOW, f32)
-        acc[...] = jnp.zeros(acc.shape, f32)
         cs, nc, ns, nn = (info[TB0 + pair * 4 + i] for i in range(4))
+
+        @pl.when(nc + nn == 0)
+        def _():
+            mx[...] = jnp.full(mx.shape, LOW, f32)
+            acc[...] = jnp.zeros(acc.shape, f32)
+
 
         def place(j):
             return pl.multiple_of(jnp.where(j < nc, cs + j * CHUNK, ns + (j - nc) * CHUNK), 128)
@@ -203,7 +207,7 @@
                         qs[pair, pl.ds(h * ROWS, SUB1), :], keys, (((1,), (1,)), ((), ())), preferred_element_type=f32
                     )
                 rows = pl.ds(h * ROWS, ROWS)
-                best = mx[rows, :]
+                best = jnp.where(j == 0, LOW, mx[rows, :])
                 for g in range(units * CHUNK // 128):
                     part = s[low : low + ROWS, g * 128 : (g + 1) * 128] * SCALE2 + bias[h // 8][g]
                     ss[j + g // 2, rows, (g % 2) * 128 : (g % 2 + 1) * 128] = part
@@ -245,7 +249,8 @@
                     parts.append(p.astype(bf16))
                 probs.append(jnp.concatenate(parts, axis=1))
                 if len(probs) * ROWS == SUB2:
-                    acc[pl.ds((h + 1) * ROWS - SUB2, SUB2), :] += lax.dot_general(
+                    some = pl.ds((h + 1) * ROWS - SUB2, SUB2)
+                    acc[some, :] = jnp.where(j == 0, 0.0, acc[some, :]) + lax.dot_general(
                         jnp.concatenate(probs, axis=0), v, (((1,), (0,)), ((), ())), preferred_element_type=f32
                     )
                     probs = []

time: 82.2 us -> 81.8 us (level)
  the two profiles are of different devices: /device:TPU:56 before, /device:TPU:24 now
where the time goes in v7:
time: 81.8 us; the launch traced here: 80.8 us
  starting transfers between devices  31.7 us (39%)
  blocking collectives  20.6 us (25%)
  Pallas kernels  15.1 us (18%)
  waiting for transfers between devices  13.1 us (16%)
    all_to_all x1, blocking collectives, body(): parts = lax.all_to_all(partial, ('z0', 'xl', 'xh'), 0, 0)  20.6 us
    all_to_all x1, starting transfers between devices, body(): held = lax.all_to_all(slots, ('y', 'zh', 'z0'), 0, 0)  15.6 us
    ppermute x3, starting transfers between devices, body(): lax.ppermute(pair, ('xh', 'xl'), [(i, i ^ d) for i in range(4)])  9.82 us
    pallas_call x1, Pallas kernels, attend(): pl.pallas_call(attend_kernel, out_shape=jax.ShapeDtypeStruct((GROUP, PIEC...  8.79 us
    ppermute x3, waiting for transfers between devices, body(): lax.ppermute(pair, ('xh', 'xl'), [(i, i ^ d) for i in range(4)])  5.5 us
    all_to_all x1, waiting for transfers between devices, body(): held = lax.all_to_all(slots, ('y', 'zh', 'z0'), 0, 0)  5.37 us
    ppermute x1, starting transfers between devices, body(): across = lax.ppermute(queries, 'z0', [(0, 1), (1, 0)])  4.4 us
    pallas_call x1, Pallas kernels, body(): pl.pallas_call(prep_kernel, out_shape=(jax.ShapeDtypeStruct((META, 128),...  3.09 us
  transfers between devices with their start and end apart: 6, of which 5 were waited for; matrix products, arithmetic and copies ran while one was open for 0% of the time, Pallas kernels for 6%

profile of v7, /device:TPU:24, one launch (start us, length us, event | category | flops | bytes accessed | tf_op | source)
XLA Modules:
  0.0 80.8 jit_solution(2735378561655619219)
XLA Ops:
  0.0 0.0 copy-start.2
  0.0 4.4 %collective-permute-start = (bf16[128,512]{1,0:T(8,128)(2,1)}, bf16[128,512]{1,0:T(8,128)(2,1)S(1)}, u32[]{:S(2)}, u32[]{:S(2)}) collective-permute-start(bf16[128,512]{1,0:T(8,128)(2,1)} %param.7), channel_id=1, source_target_pairs={{0,4},{4,0},{1,5},{5,1},{2,6},{6,2},{3,7},{7,3},{8,12},{12,8},{9,1... | collective-permute-start | bytes 393224 | tf_op jit(solution)/shard_map/ppermute | solution.py:326
  4.4 1.8 %slots.1 = bf16[64,48,128]{2,1,0:T(8,128)(2,1)} custom-call(bf16[128,128]{1,0:T(8,128)(2,1)} %new_keys.1, bf16[128,128]{1,0:T(8,128)(2,1)} %new_values.1, bf16[64,128]{1,0:T(8,128)(2,1)} %cache_keys.1, bf16[64,128]{1,0:T(8,128)(2,1)} %cache_values.1), custom_call_target="tpu_custom_call" | custom-call | flops 1000000 | bytes 4000000 | tf_op jit(solution)/shard_map/slots/pallas_call | solution.py:327
  6.2 0.0 copy-start
  6.2 0.0 copy-start.1
  6.2 15.6 %all-to-all-start = ((bf16[64,48,128]{2,1,0:T(8,128)(2,1)}), bf16[64,48,128]{2,1,0:T(8,128)(2,1)S(1)}, u32[]{:S(2)}, u32[]{:S(2)}) async-start(bf16[64,48,128]{2,1,0:T(8,128)(2,1)} %slots.1), calls=%async_computation | async-start | bytes 1572864 | tf_op jit(solution)/shard_map/all_to_all | solution.py:336
  21.8 0.0 copy-done.2
  21.8 0.0 collective-permute-done
  21.9 4.7 %collective-permute-start.3 = (bf16[256,512]{1,0:T(8,128)(2,1)S(1)}, bf16[256,512]{1,0:T(8,128)(2,1)S(1)}, u32[]{:S(2)}, u32[]{:S(2)}) collective-permute-start(bf16[256,512]{1,0:T(8,128)(2,1)S(1)} %constant_dynamic-update-slice_fusion.refs_0_), channel_id=1, source_target_pairs={{0,258},{2,256},{256,2},{258,0},{1,259},{3,257},{257,3},{259,1},{4... | collective-permute-start | bytes 786440 | tf_op jit(solution)/shard_map/ppermute | solution.py:337
  26.5 2.7 %collective-permute-start.2 = (bf16[256,512]{1,0:T(8,128)(2,1)S(1)}, bf16[256,512]{1,0:T(8,128)(2,1)S(1)}, u32[]{:S(2)}, u32[]{:S(2)}) collective-permute-start(bf16[256,512]{1,0:T(8,128)(2,1)S(1)} %constant_dynamic-update-slice_fusion.refs_0_), channel_id=1, source_target_pairs={{0,256},{2,258},{256,0},{258,2},{1,257},{3,259},{257,1},{259,3},{4... | collective-permute-start | bytes 786440 | tf_op jit(solution)/shard_map/ppermute | solution.py:337
  29.3 2.4 %collective-permute-start.1 = (bf16[256,512]{1,0:T(8,128)(2,1)S(1)}, bf16[256,512]{1,0:T(8,128)(2,1)S(1)}, u32[]{:S(2)}, u32[]{:S(2)}) collective-permute-start(bf16[256,512]{1,0:T(8,128)(2,1)S(1)} %constant_dynamic-update-slice_fusion.refs_0_), channel_id=1, source_target_pairs={{0,2},{2,0},{256,258},{258,256},{1,3},{3,1},{257,259},{259,257},{4... | collective-permute-start | bytes 786440 | tf_op jit(solution)/shard_map/ppermute | solution.py:337
  31.7 0.0 copy-done
  31.7 0.0 copy-done.1
  31.7 3.1 %prep.1 = (f32[1056,128]{1,0:T(8,128)S(1)}, s32[72]{0:T(128)S(1)}) custom-call(s32[512]{0:T(512)S(1)} %copy-done.1, s32[128,128]{1,0:T(8,128)S(1)} %bitcast.1), custom_call_target="tpu_custom_call" | custom-call | flops 30000001024 | bytes 800000 | tf_op jit(solution)/shard_map/prep/pallas_call | solution.py:338
  34.8 2.1 %collective-permute-done.3.refs_3_ = bf16[256,512]{1,0:T(8,128)(2,1)S(1)} collective-permute-done((bf16[256,512]{1,0:T(8,128)(2,1)S(1)}, bf16[256,512]{1,0:T(8,128)(2,1)S(1)}, u32[]{:S(2)}, u32[]{:S(2)}) %collective-permute-start.3) | collective-permute-done | bytes 262176 | tf_op jit(solution)/shard_map/ppermute | solution.py:337
  36.9 2.3 %collective-permute-done.2.refs_2_ = bf16[256,512]{1,0:T(8,128)(2,1)S(1)} collective-permute-done((bf16[256,512]{1,0:T(8,128)(2,1)S(1)}, bf16[256,512]{1,0:T(8,128)(2,1)S(1)}, u32[]{:S(2)}, u32[]{:S(2)}) %collective-permute-start.2) | collective-permute-done | bytes 262176 | tf_op jit(solution)/shard_map/ppermute | solution.py:337
  39.2 1.1 %collective-permute-done.1.refs_1_ = bf16[256,512]{1,0:T(8,128)(2,1)S(1)} collective-permute-done((bf16[256,512]{1,0:T(8,128)(2,1)S(1)}, bf16[256,512]{1,0:T(8,128)(2,1)S(1)}, u32[]{:S(2)}, u32[]{:S(2)}) %collective-permute-start.1) | collective-permute-done | bytes 262176 | tf_op jit(solution)/shard_map/ppermute | solution.py:337
  40.3 5.4 %all-to-all-done.refs_4_ = bf16[64,48,128]{2,1,0:T(8,128)(2,1)S(1)} async-done(((bf16[64,48,128]{2,1,0:T(8,128)(2,1)}), bf16[64,48,128]{2,1,0:T(8,128)(2,1)S(1)}, u32[]{:S(2)}, u32[]{:S(2)}) %all-to-all-start) | async-done | bytes 786464 | tf_op jit(solution)/shard_map/all_to_all | solution.py:336
  45.7 1.9 %collective-permute-start.4 = (bf16[64,48,128]{2,1,0:T(8,128)(2,1)S(1)}, bf16[64,48,128]{2,1,0:T(8,128)(2,1)S(1)}, u32[]{:S(2)}, u32[]{:S(2)}) collective-permute-start(bf16[64,48,128]{2,1,0:T(8,128)(2,1)S(1)} %all-to-all-done.refs_4_), channel_id=1, source_target_pairs={{0,1},{1,0},{2,3},{3,2},{4,5},{5,4},{6,7},{7,6},{8,9},{9,8},{10,11... | collective-permute-start | bytes 2359304 | tf_op jit(solution)/shard_map/ppermute | solution.py:348
  47.6 2.3 %collective-permute-done.4.refs_5_ = bf16[64,48,128]{2,1,0:T(8,128)(2,1)S(1)} collective-permute-done((bf16[64,48,128]{2,1,0:T(8,128)(2,1)S(1)}, bf16[64,48,128]{2,1,0:T(8,128)(2,1)S(1)}, u32[]{:S(2)}, u32[]{:S(2)}) %collective-permute-start.4) | collective-permute-done | bytes 786464 | tf_op jit(solution)/shard_map/ppermute | solution.py:348
  49.9 8.8 %attend.1 = bf16[8,528,128]{2,1,0:T(8,128)(2,1)S(1)} custom-call(s32[72]{0:T(128)S(1)} %get-tuple-element.16.info_in, bf16[256,512]{1,0:T(8,128)(2,1)S(1)} %constant_dynamic-update-slice_fusion.refs_0_, bf16[256,512]{1,0:T(8,128)(2,1)S(1)} %collective-permute-done.1.refs_1_, bf16[256,512]{1,0:T(8,128)(2,1)S(1)} %collective-permute-done.2.refs_2_, ...), custom_call_target="tpu_custom_call" | custom-call | flops 4096000000 | bytes 4000000 | tf_op jit(solution)/shard_map/attend/pallas_call | solution.py:285
  58.7 20.6 %all_to_all.10.r_ref = bf16[8,528,128]{2,1,0:T(8,128)(2,1)S(1)} all-to-all(bf16[8,528,128]{2,1,0:T(8,128)(2,1)S(1)} %attend.1), channel_id=1, replica_groups=mesh['xh'=2,'y'=8,'zh'=4,'z0'=2,'xl'=2,'core'=2] {'z0','xl','xh'}, dimensions={0} | all-to-all | bytes 2162688 | tf_op jit(solution)/shard_map/all_to_all | solution.py:350
  79.3 1.5 %combine.1 = bf16[128,512]{1,0:T(8,128)(2,1)} custom-call(bf16[8,528,128]{2,1,0:T(8,128)(2,1)S(1)} %all_to_all.10.r_ref), custom_call_target="tpu_custom_call" | custom-call | tf_op jit(solution)/shard_map/combine/pallas_call | solution.py:351
  (2 shorter events, 0.0 us)
Async XLA Ops:
  0.0 21.8 %copy-start.2 = (bf16[128,512]{1,0:T(8,128)(2,1)S(1)}, bf16[128,512]{1,0:T(8,128)(2,1)}, u32[]{:S(2)}) copy-start(bf16[128,512]{1,0:T(8,128)(2,1)} %param.7) | copy-start | bytes 393220
  0.0 21.8 %collective-permute-start = (bf16[128,512]{1,0:T(8,128)(2,1)}, bf16[128,512]{1,0:T(8,128)(2,1)S(1)}, u32[]{:S(2)}, u32[]{:S(2)}) collective-permute-start(bf16[128,512]{1,0:T(8,128)(2,1)} %param.7), channel_id=1, source_target_pairs={{0,4},{4,0},{1,5},{5,1},{2,6},{6,2},{3,7},{7,3},{8,12},{12,8},{9,1... | collective-permute-start | bytes 393224 | tf_op jit(solution)/shard_map/ppermute | solution.py:326
  6.2 25.5 %copy-start = (s32[16384]{0:T(1024)S(1)}, s32[16384]{0:T(1024)}, u32[]{:S(2)}) copy-start(s32[16384]{0:T(1024)} %param.12) | copy-start | bytes 196612
  6.2 25.5 %copy-start.1 = (s32[512]{0:T(512)S(1)}, s32[512]{0:T(512)}, u32[]{:S(2)}) copy-start(s32[512]{0:T(512)} %blocks.1) | copy-start | bytes 6148
  6.2 39.5 %all-to-all-start = ((bf16[64,48,128]{2,1,0:T(8,128)(2,1)}), bf16[64,48,128]{2,1,0:T(8,128)(2,1)S(1)}, u32[]{:S(2)}, u32[]{:S(2)}) async-start(bf16[64,48,128]{2,1,0:T(8,128)(2,1)} %slots.1), calls=%async_computation | async-start | bytes 1572864 | tf_op jit(solution)/shard_map/all_to_all | solution.py:336
  21.9 15.0 %collective-permute-start.3 = (bf16[256,512]{1,0:T(8,128)(2,1)S(1)}, bf16[256,512]{1,0:T(8,128)(2,1)S(1)}, u32[]{:S(2)}, u32[]{:S(2)}) collective-permute-start(bf16[256,512]{1,0:T(8,128)(2,1)S(1)} %constant_dynamic-update-slice_fusion.refs_0_), channel_id=1, source_target_pairs={{0,258},{2,256},{256,2},{258,0},{1,259},{3,257},{257,3},{259,1},{4... | collective-permute-start | bytes 786440 | tf_op jit(solution)/shard_map/ppermute | solution.py:337
  26.5 12.6 %collective-permute-start.2 = (bf16[256,512]{1,0:T(8,128)(2,1)S(1)}, bf16[256,512]{1,0:T(8,128)(2,1)S(1)}, u32[]{:S(2)}, u32[]{:S(2)}) collective-permute-start(bf16[256,512]{1,0:T(8,128)(2,1)S(1)} %constant_dynamic-update-slice_fusion.refs_0_), channel_id=1, source_target_pairs={{0,256},{2,258},{256,0},{258,2},{1,257},{3,259},{257,1},{259,3},{4... | collective-permute-start | bytes 786440 | tf_op jit(solution)/shard_map/ppermute | solution.py:337
  29.3 11.1 %collective-permute-start.1 = (bf16[256,512]{1,0:T(8,128)(2,1)S(1)}, bf16[256,512]{1,0:T(8,128)(2,1)S(1)}, u32[]{:S(2)}, u32[]{:S(2)}) collective-permute-start(bf16[256,512]{1,0:T(8,128)(2,1)S(1)} %constant_dynamic-update-slice_fusion.refs_0_), channel_id=1, source_target_pairs={{0,2},{2,0},{256,258},{258,256},{1,3},{3,1},{257,259},{259,257},{4... | collective-permute-start | bytes 786440 | tf_op jit(solution)/shard_map/ppermute | solution.py:337
  45.7 4.2 %collective-permute-start.4 = (bf16[64,48,128]{2,1,0:T(8,128)(2,1)S(1)}, bf16[64,48,128]{2,1,0:T(8,128)(2,1)S(1)}, u32[]{:S(2)}, u32[]{:S(2)}) collective-permute-start(bf16[64,48,128]{2,1,0:T(8,128)(2,1)S(1)} %all-to-all-done.refs_4_), channel_id=1, source_target_pairs={{0,1},{1,0},{2,3},{3,2},{4,5},{5,4},{6,7},{7,6},{8,9},{9,8},{10,11... | collective-permute-start | bytes 2359304 | tf_op jit(solution)/shard_map/ppermute | solution.py:348
